TPU v7x, 256 devices: a whole 4x4x8 slice. The times are simulated.
256 devices in a mesh: seg: 64 (over x, z, core), det: 4 (over y).
Axes of the slice: x: 4, y: 4, z: 8, core: 2. Of those that a mesh axis runs over, the one named last changes fastest.
Arguments:
- strain: float32 [4, 64, 4096], P('det', 'seg'), may hold values from -6 to 6
- antenna: float32 [2, 4], replicated, may hold values from -1 to 1
- delays: int32 [4], replicated, may hold values from -24 to 24
- template_bank: bfloat16 [64, 256, 4096], P('seg', 'det'), may hold values from -6 to 6
- duration_bin: int32 [64, 256], P('seg', 'det'), may hold values from 0 to 7
- owner_seg: int32 [64, 2048, 1], P('seg', 'det'), may hold values from 0 to 63; in each aligned block of 512 rows (0 to 511, 512 to 1023, ..., all dimensions but the last counted through in order) at most 16 rows name the same one
- slot_index: int32 [64, 2048], P('seg', 'det'), may hold values from 0 to 63
Outputs:
- snr_squared: float32 [64, 2048, 1024], P('seg', 'det')
Inputs may be any that keep to these rules, and one draw needn't show every extreme that they name: `owner_seg`: in each device's rows of 512 requests no owner is named more than 16 times, a bound that some block reaches.
All inputs are finite; a program needn't handle non-finite values.
Results may differ from a plain program's by a relative error of at most 0.0031.
Values may be sent and summed in bfloat16 or wider, within the bound.
No kernel may reach another device: no remote copies, remote signals or barrier semaphores. Data moves between devices by JAX's collectives and lax.ppermute only.
A program may use at most 128 MiB of HBM per device.

v0:
```python
import functools
import math

import jax
import jax.numpy as jnp
import numpy as np
from jax import lax
from jax.experimental import pallas as pl
from jax.experimental.pallas import tpu as pltpu
from jax.sharding import PartitionSpec as P

HALF = 2048
WIDE = 2 * HALF
STEP = 1024
NX, NZ, NC = 4, 8, 2
PEERS = NX * NC
ND = 4
CAP = 16
SLOTS = 64
CLASSES = 16
T1 = 256
QS = 4
BIG = 3.0e38
CALLS = {(0, -1, 1, -2, 2): ((0, -1, 1), (-2, 2)), (-3, 3, 4): ((-3, 3, 4),)}
PARTS = tuple(CALLS)

LANE = np.arange(128)
FREQ = 128 * (LANE % 16)[None, :] + 16 * (LANE // 16)[None, :] + np.arange(CLASSES)[:, None]


def class_basis():
    t = np.arange(T1)
    ang = ((FREQ[:, :, None] * t[None, None, :]) % WIDE) * (math.pi / HALF)
    c, s = np.cos(ang), np.sin(ang)
    upper = np.concatenate([c, s], 2)
    lower = np.concatenate([-s, c], 2)
    return np.concatenate([upper, lower], 1).astype(np.float32).astype(jnp.bfloat16)


def to_classes(x, lane):
    for k in range(4):
        b = 1 << k
        up = (lane & b) != 0
        for g in range(16):
            if g & b:
                continue
            lo, hi = x[g], x[g | b]
            x[g] = jnp.where(up, pltpu.roll(hi, b, 1), lo)
            x[g | b] = jnp.where(up, hi, pltpu.roll(lo, 128 - b, 1))
    return x


def lookup(dz, values):
    out = jnp.zeros_like(dz)
    for d, v in enumerate(values):
        if v:
            out = jnp.where(dz == d, v, out)
    return out


def head_kernel(delays_ref, strain_ref, owner_ref, slot_ref, packet_ref, place_ref):
    det, my_z = lax.axis_index("det"), (lax.axis_index("seg") // NC) % NZ
    owner = owner_ref[...]
    n = owner.shape[1]
    peer = (owner // (NZ * NC)) * NC + (owner & 1)
    dz = ((owner >> 1) - my_z) & (NZ - 1)
    part_of, order_of, first_of = [0] * NZ, [0] * NZ, [0] * NZ
    first = 0
    for g, part in enumerate(PARTS):
        for j, d in enumerate(part):
            part_of[d % NZ], order_of[d % NZ], first_of[d % NZ] = g, j, first
        first += len(part) * CAP
    hot = owner == lax.broadcasted_iota(jnp.int32, (PEERS * NZ, n), 0)
    earlier = lax.broadcasted_iota(jnp.int32, (n, n), 0) < lax.broadcasted_iota(jnp.int32, (n, n), 1)
    before = jnp.dot(
        hot.astype(jnp.float32).astype(jnp.bfloat16),
        earlier.astype(jnp.float32).astype(jnp.bfloat16),
        preferred_element_type=jnp.float32,
    )
    rank = jnp.sum(jnp.where(hot, before, 0.0), axis=0, keepdims=True).astype(jnp.int32)
    start = lookup(dz, first_of)
    rank = rank + CAP * lookup(dz, order_of)
    want = (slot_ref[...] + 1).astype(jnp.float32)
    size = lookup(dz, [len(PARTS[g]) * CAP for g in part_of])
    place = (start * PEERS + peer * size + rank).astype(jnp.float32)
    place_ref[...] = jnp.transpose(jnp.broadcast_to(place, (8, n)))
    wanted = jnp.where(peer == lax.broadcasted_iota(jnp.int32, (PEERS, n), 0), want, 0.0)
    spot = (start + rank) == lax.broadcasted_iota(jnp.int32, (NZ * CAP, n), 0)
    table = (
        lax.dot_general(
            wanted.astype(jnp.bfloat16),
            spot.astype(jnp.float32).astype(jnp.bfloat16),
            (((1,), (1,)), ((), ())),
            preferred_element_type=jnp.float32,
        )
        - 1.0
    )

    delay = delays_ref[det]
    row16 = lax.broadcasted_iota(jnp.int32, (16, 128), 0)
    lane16 = lax.broadcasted_iota(jnp.int32, (16, 128), 1)
    freq = row16 * 128 + lane16
    phase = ((freq * delay) & (WIDE - 1)).astype(jnp.float32) * (-math.pi / HALF)
    cos_rot, sin_rot = jnp.cos(phase), jnp.sin(phase)
    re, im = strain_ref[0:16, :], strain_ref[16:32, :]
    lane1 = lax.broadcasted_iota(jnp.int32, (1, 128), 1)
    for c, x in enumerate((re * cos_rot - im * sin_rot, re * sin_rot + im * cos_rot)):
        x = to_classes([x[g : g + 1, :] for g in range(16)], lane1)
        for f2 in range(CLASSES):
            at = f2 * 256 + c * 128
            packet_ref[0, :, at : at + 128] = x[f2]
    shifted = packet_ref[0, :, 0:WIDE]
    for m in range(PEERS * ND):
        if m:
            packet_ref[m, :, 0:WIDE] = shifted
        packet_ref[m, :, WIDE:] = table[m // ND : m // ND + 1, :]


def bank_kernel(dur_ref, bank_ref, out_ref):
    row16 = lax.broadcasted_iota(jnp.int32, (16, 128), 0)
    lane16 = lax.broadcasted_iota(jnp.int32, (16, 128), 1)

    def rows(i, _):
        r = pl.ds(pl.multiple_of(i * 16, 16), 16)
        dur = jnp.zeros((16, 128), jnp.int32)
        for j in range(16):
            dur = jnp.where(row16 == j, dur_ref[0, i * 16 + j], dur)
        for c in range(2):
            x = []
            for g in range(16):
                v = bank_ref[r, c * HALF + g * 128 : c * HALF + (g + 1) * 128].astype(jnp.float32)
                x.append(jnp.where(dur <= g, v, 0.0))
            x = to_classes(x, lane16)
            for f2 in range(CLASSES):
                at = f2 * 256 + c * 128
                out_ref[r, at : at + 128] = x[f2].astype(jnp.bfloat16)
        return 0

    lax.fori_loop(0, SLOTS // 16, rows, 0)


def head(delays, strain, owner, slot):
    n = owner.shape[1]
    vmem = pl.BlockSpec(memory_space=pltpu.VMEM)
    smem = pl.BlockSpec(memory_space=pltpu.SMEM)
    return pl.pallas_call(
        head_kernel,
        out_shape=[
            jax.ShapeDtypeStruct((PEERS * ND, 1, WIDE + 128), jnp.float32),
            jax.ShapeDtypeStruct((n, 8), jnp.float32),
        ],
        in_specs=[smem] + [vmem] * 3,
        out_specs=[vmem] * 2,
        compiler_params=pltpu.CompilerParams(vmem_limit_bytes=58 << 20),
        cost_estimate=pl.CostEstimate(flops=4 << 20, bytes_accessed=2 << 20, transcendentals=0),
        name="head",
    )(delays, strain, owner, slot)


def prepare_bank(dur, bank):
    vmem = pl.BlockSpec(memory_space=pltpu.VMEM)
    return pl.pallas_call(
        bank_kernel,
        out_shape=jax.ShapeDtypeStruct((SLOTS, WIDE), jnp.bfloat16),
        in_specs=[pl.BlockSpec(memory_space=pltpu.SMEM), vmem],
        out_specs=vmem,
        compiler_params=pltpu.CompilerParams(vmem_limit_bytes=58 << 20),
        cost_estimate=pl.CostEstimate(flops=4 << 20, bytes_accessed=2 << 20, transcendentals=0),
        name="prepare_bank",
    )(dur, bank)


def combine_kernel(antenna_ref, packet_ref, out_ref):
    det = lax.axis_index("det")
    for s in range(PEERS):
        rows = [packet_ref[s * ND + d, :, 0:WIDE] for d in range(ND)]
        for p in range(2):
            total = antenna_ref[p, 0] * rows[0]
            for d in range(1, ND):
                total = total + antenna_ref[p, d] * rows[d]
            out_ref[s, :, p * WIDE : (p + 1) * WIDE] = total
        out_ref[s, :, 2 * WIDE :] = packet_ref[s * ND + det, :, WIDE:]


def combine(antenna, packet):
    vmem = pl.BlockSpec(memory_space=pltpu.VMEM)
    smem = pl.BlockSpec(memory_space=pltpu.SMEM)
    return pl.pallas_call(
        combine_kernel,
        out_shape=jax.ShapeDtypeStruct((PEERS, 1, 2 * WIDE + 128), jnp.float32),
        in_specs=[smem, vmem],
        out_specs=vmem,
        compiler_params=pltpu.CompilerParams(vmem_limit_bytes=16 << 20),
        cost_estimate=pl.CostEstimate(flops=1 << 20, bytes_accessed=1 << 20, transcendentals=0),
        name="combine",
    )(antenna, packet)


def rotate(re, im, k):
    k %= 16
    if k == 0:
        return re, im
    if k == 4:
        return -im, re
    if k == 8:
        return -re, -im
    if k == 12:
        return im, -re
    c, s = math.cos(math.pi * k / 8), math.sin(math.pi * k / 8)
    return re * c - im * s, re * s + im * c


def cadd(a, b):
    return a[0] + b[0], a[1] + b[1]


def csub(a, b):
    return a[0] - b[0], a[1] - b[1]


def lags_of(load):
    def four(a):
        x0, x1, x2, x3 = load(a), load(a + 4), load(a + 8), load(a + 12)
        e0, e1, o0, o1 = cadd(x0, x2), csub(x0, x2), cadd(x1, x3), csub(x1, x3)
        turned = (-o1[1], o1[0])
        return [cadd(e0, o0), cadd(e1, turned), csub(e0, o0), csub(e1, turned)]

    def pair(a):
        y, z = four(a), four(a + 2)
        return [cadd(y[q], rotate(*z[q], 2 * q)) for q in range(QS)]

    even, odd = pair(0), pair(1)
    return [cadd(even[q], rotate(*odd[q], q)) for q in range(QS)]


def stage_kernel(source, out_ref, sem):
    copy = pltpu.make_async_copy(source, out_ref, sem)
    copy.start()
    copy.wait()


def stage(basis):
    return pl.pallas_call(
        stage_kernel,
        out_shape=jax.ShapeDtypeStruct(basis.shape, basis.dtype),
        in_specs=[pl.BlockSpec(memory_space=pl.ANY)],
        out_specs=pl.BlockSpec(memory_space=pltpu.VMEM),
        scratch_shapes=[pltpu.SemaphoreType.DMA],
        compiler_params=pltpu.CompilerParams(vmem_limit_bytes=16 << 20),
        cost_estimate=pl.CostEstimate(flops=0, bytes_accessed=8 << 20, transcendentals=0),
        name="stage_basis",
    )(basis)


def filter_kernel(count, first, slot, *refs):
    banks = refs[:count]
    packet_ref, basis_ref, _, whole_ref, token_ref, bank, column, coh, spec, xs, norms, out_ref, bank_sems, out_sem = refs[count:]
    half = PEERS * CAP
    loads = [pltpu.make_async_copy(banks[i], bank.at[i], bank_sems.at[i]) for i in range(count)]
    for load in loads:
        load.start()
    table = jnp.concatenate([packet_ref[s, :, 2 * WIDE : 2 * WIDE + 128] for s in range(PEERS)], 0)
    column[...] = jnp.transpose(table)
    for s in range(PEERS):
        for p in range(2):
            coh[2 * s + p : 2 * s + p + 1, :] = packet_ref[s, :, p * WIDE : (p + 1) * WIDE]
    lane = lax.broadcasted_iota(jnp.int32, (CAP, SLOTS), 1).astype(jnp.float32)

    def block(i, _):
        for j in range(count):

            @pl.when(i == j)
            def _(j=j):
                loads[j].wait()

        want = column[pl.ds(pl.multiple_of(first + i * CAP, CAP), CAP), :]
        hot = jnp.concatenate(
            [(want[:, s : s + 1] == lane).astype(jnp.float32) for s in range(PEERS)], 0
        ).astype(jnp.bfloat16)
        for f2 in range(CLASSES):
            at = f2 * 256
            xs[f2, :half, :256] = jnp.dot(
                hot, bank[i, :, at : at + 256], preferred_element_type=jnp.float32
            )
        square = jnp.zeros((half, 128), jnp.float32)
        for f2 in range(CLASSES):
            at = f2 * 256
            tr, ti = xs[f2, :half, :128], xs[f2, :half, 128:256]
            square = square + (tr * tr + ti * ti)
            for s in range(PEERS):
                rs = slice(s * CAP, (s + 1) * CAP)
                trs, tis = tr[rs], ti[rs]
                for p in range(2):
                    nr = coh[2 * s + p : 2 * s + p + 1, at : at + 128]
                    ni = coh[2 * s + p : 2 * s + p + 1, at + 128 : at + 256]
                    to = slice(p * half + s * CAP, p * half + (s + 1) * CAP)
                    spec[f2, to, 0:128] = (nr * trs + ni * tis).astype(jnp.bfloat16)
                    spec[f2, to, 128:256] = (ni * trs - nr * tis).astype(jnp.bfloat16)
        norms[...] = jnp.broadcast_to(jnp.sum(square, axis=1, keepdims=True), (half, 128))

        for f2 in range(CLASSES):
            xs[f2] = jnp.dot(spec[f2], basis_ref[f2], preferred_element_type=jnp.float32)

        def tile(s, _):
            row = pl.multiple_of(s * CAP, CAP)
            norm = norms[pl.ds(row, CAP), :]
            good = norm > 0.0
            scale = jnp.where(good, 1.0 / jnp.where(good, norm, 1.0), 0.0)
            offset = jnp.where(good, 0.0, -1.0)
            for h in range(T1 // 128):
                parts = [[] for _ in range(QS)]
                for u in range(CAP // 8):
                    power = [None] * QS
                    for p in range(2):
                        rows = pl.ds(p * half + row + 8 * u, 8)

                        def load(f2, rows=rows, h=h):
                            return (
                                xs[f2, rows, h * 128 : (h + 1) * 128],
                                xs[f2, rows, T1 + h * 128 : T1 + (h + 1) * 128],
                            )

                        for q, (re, im) in enumerate(lags_of(load)):
                            w = re * re + im * im
                            power[q] = w if p == 0 else power[q] + w
                    for q in range(QS):
                        v = power[q] * scale[8 * u : 8 * u + 8] + offset[8 * u : 8 * u + 8]
                        parts[q].append(jnp.minimum(v, BIG))
                for q in range(QS):
                    v = jnp.concatenate(parts[q], 0).astype(jnp.bfloat16)
                    out_ref[s, i, :, q * T1 + h * 128 : q * T1 + (h + 1) * 128] = v
            return 0

        lax.fori_loop(0, PEERS, tile, 0, unroll=2)
        return 0

    lax.fori_loop(0, count, block, 0)
    put = pltpu.make_async_copy(out_ref, whole_ref.at[:, pl.ds(slot, count)], out_sem)
    put.start()
    token_ref[...] = norms[0:8, :]
    put.wait()


def filter_banks(banks, first, packet, basis, slot, total, before):
    count = len(banks)
    vmem = pl.BlockSpec(memory_space=pltpu.VMEM)
    any_space = pl.BlockSpec(memory_space=pl.ANY)
    half = PEERS * CAP
    return pl.pallas_call(
        functools.partial(filter_kernel, count, first, slot),
        out_shape=[
            jax.ShapeDtypeStruct((PEERS, total, CAP, STEP), jnp.bfloat16),
            jax.ShapeDtypeStruct((8, 128), jnp.float32),
        ],
        in_specs=[any_space] * count + [vmem, vmem, any_space],
        out_specs=[any_space, vmem],
        input_output_aliases={count + 2: 0} if slot else {},
        scratch_shapes=[
            pltpu.VMEM((count, SLOTS, WIDE), jnp.bfloat16),
            pltpu.VMEM((128, PEERS), jnp.float32),
            pltpu.VMEM((2 * PEERS, WIDE), jnp.float32),
            pltpu.VMEM((CLASSES, 2 * half, 256), jnp.bfloat16),
            pltpu.VMEM((CLASSES, 2 * half, 2 * T1), jnp.float32),
            pltpu.VMEM((half, 128), jnp.float32),
            pltpu.VMEM((PEERS, count, CAP, STEP), jnp.bfloat16),
            pltpu.SemaphoreType.DMA((count,)),
            pltpu.SemaphoreType.DMA,
        ],
        compiler_params=pltpu.CompilerParams(vmem_limit_bytes=24 << 20),
        cost_estimate=pl.CostEstimate(
            flops=count * (3 << 30), bytes_accessed=(5 << 20) + count * (1 << 20), transcendentals=0
        ),
        name=f"filter{count}_{first}",
    )(*banks, packet, basis, before)


def order_kernel(sizes, *refs):
    rows = refs[: len(sizes)]
    place_ref, out_ref = refs[len(sizes) :]
    out, first = None, 0
    for n, ref in zip(sizes, rows):
        lane = first + lax.broadcasted_iota(jnp.int32, (place_ref.shape[0], n), 1)
        pick = (place_ref[:, 0:1] == lane.astype(jnp.float32)).astype(jnp.bfloat16)
        part = jnp.dot(pick, ref[...], preferred_element_type=jnp.float32)
        out = part if out is None else out + part
        first += n
    out_ref[...] = jnp.where(out < 0.0, jnp.nan, out)


def order_rows(rows, place):
    n = place.shape[0]
    step = 128
    return pl.pallas_call(
        functools.partial(order_kernel, [r.shape[0] for r in rows]),
        out_shape=jax.ShapeDtypeStruct((n, STEP), jnp.float32),
        grid=(n // step,),
        in_specs=[pl.BlockSpec(r.shape, lambda i: (0, 0)) for r in rows]
        + [pl.BlockSpec((step, 8), lambda i: (i, 0))],
        out_specs=pl.BlockSpec((step, STEP), lambda i: (i, 0)),
        compiler_params=pltpu.CompilerParams(vmem_limit_bytes=24 << 20),
        cost_estimate=pl.CostEstimate(flops=1 << 30, bytes_accessed=4 << 20, transcendentals=0),
        name="order_rows",
    )(*rows, place)


def per_device(basis, strain, antenna, delays, template_bank, duration_bin, owner_seg, slot_index):
    def at(x, z, c):
        return (x * NZ + z) * NC + c

    places = [(x, z, c) for x in range(NX) for z in range(NZ) for c in range(NC)]
    groups = [[at(x, z, c) for x in range(NX) for c in range(NC)] for z in range(NZ)]
    up = [(at(x, z, c), at(x, (z + 1) % NZ, c)) for x, z, c in places]
    down = [(at(x, z, c), at(x, (z - 1) % NZ, c)) for x, z, c in places]
    groups = [[i * ND + d for i in group for d in range(ND)] for group in groups]
    back_groups = [[at(x, z, c) for x in range(NX) for c in range(NC)] for z in range(NZ)]
    half = SLOTS // 2

    with jax.named_scope("head"):
        own = prepare_bank(duration_bin, template_bank[0])
        own, strain = lax.optimization_barrier((own, strain))
        packet, place = head(
            delays, strain.reshape(WIDE // 128, 128), owner_seg.reshape(1, -1), slot_index
        )

    held = {0: own}

    def ring(k):
        with jax.named_scope("ring"):
            if k < 4:
                held[-k] = lax.ppermute(held[1 - k], "seg", up)
                held[k] = lax.ppermute(held[k - 1], "seg", down)
            else:
                held[4] = jnp.concatenate(
                    [lax.ppermute(held[-3][:half], "seg", up), lax.ppermute(held[3][half:], "seg", down)], 0
                )

    ring(1)
    with jax.named_scope("exchange"):
        packet = lax.all_to_all(
            packet, ("seg", "det"), split_axis=0, concat_axis=0, tiled=True, axis_index_groups=groups
        )
        packet, held[1], held[-1] = lax.optimization_barrier((packet, held[1], held[-1]))
        packet = combine(antenna, packet)
        basis = stage(basis)
    ring(2)

    back, first, token = [], 0, place
    for part in PARTS:
        m = len(part)
        rows, slot = token, 0
        for step in CALLS[part]:
            with jax.named_scope("filter"):
                rows, token = filter_banks(
                    [held[d] for d in step], first + slot * CAP, packet, basis, slot, m, rows
                )
            slot += len(step)
            k = max(held)
            if k < 4:
                token, held[k], held[-k] = lax.optimization_barrier((token, held[k], held[-k]))
                ring(k + 1)
        first += m * CAP
        with jax.named_scope("back"):
            rows = lax.all_to_all(
                rows.reshape(PEERS, m * CAP, STEP),
                "seg",
                split_axis=0,
                concat_axis=0,
                tiled=True,
                axis_index_groups=back_groups,
            )
        back.append(rows.reshape(PEERS * m * CAP, STEP))
    with jax.named_scope("order"):
        return order_rows(back, place)[None]


def solution(mesh):
    basis = class_basis()
    in_specs = (
        P("det", "seg", None),
        P(),
        P(),
        P("seg", "det", None),
        P("seg", "det"),
        P("seg", "det", None),
        P("seg", "det"),
    )

    def run(*args):
        return jax.shard_map(
            lambda *a: per_device(jnp.asarray(basis), *a),
            mesh=mesh,
            in_specs=in_specs,
            out_specs=P("seg", "det", None),
            check_vma=False,
        )(*args)

    return run
```

profile of v0, /device:TPU:1, one launch (start us, length us, event | category | flops | bytes accessed | tf_op | source)
XLA Modules:
  0.0 111.9 jit_solution(10086779633470831241)
XLA Ops:
  0.0 3.2 %prepare_bank.1.refs_0_ = bf16[64,4096]{1,0:T(8,128)(2,1)} custom-call(s32[1,64]{1,0:T(1,128)} %dur_ref.1, bf16[64,4096]{1,0:T(8,128)(2,1)} %bitcast.11), custom_call_target="tpu_custom_call" | custom-call | flops 4194304 | bytes 2097152 | tf_op jit(solution)/shard_map/head/prepare_bank/pallas_call | solution.py:162
  3.2 6.4 %collective-permute-start = (bf16[64,4096]{1,0:T(8,128)(2,1)}, bf16[64,4096]{1,0:T(8,128)(2,1)S(1)}, u32[]{:S(2)}, u32[]{:S(2)}) collective-permute-start(bf16[64,4096]{1,0:T(8,128)(2,1)} %prepare_bank.1.refs_0_), channel_id=1, source_target_pairs={{0,56},{4,60},{8,0},{12,4},{16,8},{20,12},{24,16},{28,20},{32,24},... | collective-permute-start | bytes 1572872 | tf_op jit(solution)/shard_map/ring/ppermute | solution.py:431
  9.6 0.0 collective-permute-start.1
  9.6 2.1 %head.1 = (f32[32,1,4224]{2,1,0:T(1,128)}, f32[512,8]{1,0:T(8,128)}) custom-call(s32[4]{0:T(128)} %delays_ref.1, f32[32,128]{1,0:T(8,128)} %bitcast.12, s32[1,512]{1,0:T(1,128)} %bitcast.13, s32[1,512]{1,0:T(1,128)} %slot_ref.1), custom_call_target="tpu_custom_call" | custom-call | flops 4194304 | bytes 2097152 | tf_op jit(solution)/shard_map/head/head/pallas_call | solution.py:146
  11.8 8.0 %all-to-all-start = ((f32[32,1,4224]{2,1,0:T(1,128)}), f32[32,1,4224]{2,1,0:T(1,128)S(1)}, u32[]{:S(2)}, u32[]{:S(2)}) async-start(f32[32,1,4224]{2,1,0:T(1,128)} %get-tuple-element.22), calls=%async_computation | async-start | bytes 1081344 | tf_op jit(solution)/shard_map/exchange/all_to_all | solution.py:439
  19.8 0.0 copy-start.4
  19.8 2.2 %copy-done.4 = bf16[16,256,512]{2,1,0:T(8,128)(2,1)S(1)} copy-done((bf16[16,256,512]{2,1,0:T(8,128)(2,1)S(1)}, bf16[16,256,512]{2,1,0:T(8,128)(2,1)}, u32[]{:S(2)}) %copy-start.4) | copy-done | bytes 4194328
  22.0 0.3 stage_basis.1.refs_4_.refs_3_
  22.3 1.9 %copy-done = bf16[16,256,512]{2,1,0:T(8,128)(2,1)} copy-done((bf16[16,256,512]{2,1,0:T(8,128)(2,1)}, bf16[16,256,512]{2,1,0:T(8,128)(2,1)S(1)}, u32[]{:S(2)}) %copy-start) | copy-done | bytes 4194328
  24.3 6.7 %all-to-all-done.packet_ref = f32[32,1,4224]{2,1,0:T(1,128)S(1)} async-done(((f32[32,1,4224]{2,1,0:T(1,128)}), f32[32,1,4224]{2,1,0:T(1,128)S(1)}, u32[]{:S(2)}, u32[]{:S(2)}) %all-to-all-start) | async-done | bytes 540704 | tf_op jit(solution)/shard_map/exchange/all_to_all | solution.py:439
  31.0 0.0 collective-permute-done.refs_2_
  31.0 0.0 collective-permute-done.1.refs_1_
  31.0 3.0 %collective-permute-start.2 = (bf16[64,4096]{1,0:T(8,128)(2,1)S(1)}, bf16[64,4096]{1,0:T(8,128)(2,1)S(1)}, u32[]{:S(2)}, u32[]{:S(2)}) collective-permute-start(bf16[64,4096]{1,0:T(8,128)(2,1)S(1)} %collective-permute-done.refs_2_), channel_id=1, source_target_pairs={{0,56},{4,60},{8,0},{12,4},{16,8},{20,12},{24,16},{28,20},{32,24},... | collective-permute-start | bytes 1572872 | tf_op jit(solution)/shard_map/ring/ppermute | solution.py:431
  34.0 0.0 collective-permute-start.3
  34.0 0.6 combine.1.refs_3_.refs_2_
  34.6 2.2 %copy-done.1 = bf16[16,256,512]{2,1,0:T(8,128)(2,1)S(1)} copy-done((bf16[16,256,512]{2,1,0:T(8,128)(2,1)S(1)}, bf16[16,256,512]{2,1,0:T(8,128)(2,1)}, u32[]{:S(2)}) %copy-start.1) | copy-done | bytes 4194328
  36.8 12.3 %filter3_0.1 = (bf16[8,5,16,1024]{3,2,1,0:T(8,128)(2,1)}, f32[8,128]{1,0:T(8,128)}) custom-call(bf16[64,4096]{1,0:T(8,128)(2,1)S(1)} %copy-done.5, bf16[64,4096]{1,0:T(8,128)(2,1)S(1)} %collective-permute-done.1.refs_1_, bf16[64,4096]{1,0:T(8,128)(2,1)S(1)} %collective-permute-done.refs_2_, f32[8,1,8320]{2,1,0:T(1,128)S(1)} %combine.1.refs_3_.refs_2_, ...), custom_call_target="tpu_custom_call" | custom-call | flops 9663676416 | bytes 8388608 | tf_op jit(solution)/shard_map/filter/filter3_0/pallas_call | solution.py:349
  49.1 0.0 collective-permute-done.2.refs_1_
  49.1 2.7 %collective-permute-start.4 = (bf16[64,4096]{1,0:T(8,128)(2,1)S(1)}, bf16[64,4096]{1,0:T(8,128)(2,1)S(1)}, u32[]{:S(2)}, u32[]{:S(2)}) collective-permute-start(bf16[64,4096]{1,0:T(8,128)(2,1)S(1)} %collective-permute-done.2.refs_1_), channel_id=1, source_target_pairs={{0,56},{4,60},{8,0},{12,4},{16,8},{20,12},{24,16},{28,20},{32,24},... | collective-permute-start | bytes 1572872 | tf_op jit(solution)/shard_map/ring/ppermute | solution.py:431
  51.9 8.0 %filter2_48.1 = (bf16[8,5,16,1024]{3,2,1,0:T(8,128)(2,1)}, f32[8,128]{1,0:T(8,128)S(1)}) custom-call(bf16[64,4096]{1,0:T(8,128)(2,1)S(1)} %collective-permute-done.3.refs_0_, bf16[64,4096]{1,0:T(8,128)(2,1)S(1)} %collective-permute-done.2.refs_1_, f32[8,1,8320]{2,1,0:T(1,128)S(1)} %combine.1.refs_3_.refs_2_, ...), custom_call_target="tpu_custom_call", output_to_operand_aliasing={{0}: (4, {})} | custom-call | flops 6442450944 | bytes 7340032 | tf_op jit(solution)/shard_map/filter/filter2_48/pallas_call | solution.py:349
  59.9 1.6 %collective-permute-done.4.refs_1_ = bf16[64,4096]{1,0:T(8,128)(2,1)S(1)} collective-permute-done((bf16[64,4096]{1,0:T(8,128)(2,1)S(1)}, bf16[64,4096]{1,0:T(8,128)(2,1)S(1)}, u32[]{:S(2)}, u32[]{:S(2)}) %collective-permute-start.4) | collective-permute-done | bytes 524320 | tf_op jit(solution)/shard_map/ring/ppermute | solution.py:431
  61.5 3.1 %collective-permute-done.5.refs_0_ = bf16[64,4096]{1,0:T(8,128)(2,1)S(1)} collective-permute-done((bf16[64,4096]{1,0:T(8,128)(2,1)S(1)}, bf16[64,4096]{1,0:T(8,128)(2,1)S(1)}, u32[]{:S(2)}, u32[]{:S(2)}) %collective-permute-start.5) | collective-permute-done | bytes 524320 | tf_op jit(solution)/shard_map/ring/ppermute | solution.py:430
  64.7 0.8 copy-done.7
  65.5 0.0 collective-permute-start.6
  65.5 2.9 %collective-permute-start.7 = (bf16[32,4096]{1,0:T(8,128)(2,1)S(1)}, bf16[32,4096]{1,0:T(8,128)(2,1)S(1)}, u32[]{:S(2)}, u32[]{:S(2)}) collective-permute-start(bf16[32,4096]{1,0:T(8,128)(2,1)S(1)} %slice.7), channel_id=1, source_target_pairs={{0,56},{4,60},{8,0},{12,4},{16,8},{20,12},{24,16},{28,20},{32,24},... | collective-permute-start | bytes 786440 | tf_op jit(solution)/shard_map/ring/ppermute | solution.py:434
  68.4 6.8 %all-to-all-start.1 = ((bf16[8,80,1024]{2,1,0:T(8,128)(2,1)}), bf16[8,80,1024]{2,1,0:T(8,128)(2,1)S(1)}, u32[]{:S(2)}, u32[]{:S(2)}) async-start(bf16[8,80,1024]{2,1,0:T(8,128)(2,1)} %bitcast.3), calls=%async_computation.1 | async-start | bytes 2621440 | tf_op jit(solution)/shard_map/back/all_to_all | solution.py:463
  75.3 2.2 %copy-done.3 = bf16[16,256,512]{2,1,0:T(8,128)(2,1)S(1)} copy-done((bf16[16,256,512]{2,1,0:T(8,128)(2,1)S(1)}, bf16[16,256,512]{2,1,0:T(8,128)(2,1)}, u32[]{:S(2)}) %copy-start.3) | copy-done | bytes 4194328
  77.5 1.0 copy-done.8
  78.5 11.5 %filter3_80.1 = (bf16[8,3,16,1024]{3,2,1,0:T(8,128)(2,1)S(1)}, f32[8,128]{1,0:T(8,128)}) custom-call(bf16[64,4096]{1,0:T(8,128)(2,1)S(1)} %copy-done.8, bf16[64,4096]{1,0:T(8,128)(2,1)S(1)} %collective-permute-done.4.refs_1_, bf16[64,4096]{1,0:T(8,128)(2,1)S(1)} %pad_maximum_fusion.refs_2_, f32[8,1,8320]{2,1,0:T(1,128)S(1)} %combine.1.refs_3_.refs_2_, ...), custom_call_target="tpu_custom_call" | custom-call | flops 9663676416 | bytes 8388608 | tf_op jit(solution)/shard_map/filter/filter3_80/pallas_call | solution.py:349
  90.0 3.2 %all-to-all-done.1 = bf16[8,80,1024]{2,1,0:T(8,128)(2,1)S(1)} async-done(((bf16[8,80,1024]{2,1,0:T(8,128)(2,1)}), bf16[8,80,1024]{2,1,0:T(8,128)(2,1)S(1)}, u32[]{:S(2)}, u32[]{:S(2)}) %all-to-all-start.1) | async-done | bytes 1310752 | tf_op jit(solution)/shard_map/back/all_to_all | solution.py:463
  93.1 15.5 %all_to_all.15 = bf16[8,48,1024]{2,1,0:T(8,128)(2,1)S(1)} all-to-all(bf16[8,48,1024]{2,1,0:T(8,128)(2,1)S(1)} %bitcast.10), channel_id=1, replica_groups={{0,4,64,68,128,132,192,196},{8,12,72,76,136,140,200,204},{16,20,80,84,1..., dimensions={0} | all-to-all | bytes 1572864 | tf_op jit(solution)/shard_map/back/all_to_all | solution.py:463
  108.6 3.3 %order_rows.1 = f32[512,1024]{1,0:T(8,128)} custom-call(bf16[640,1024]{1,0:T(8,128)(2,1)S(1)} %bitcast.8, bf16[384,1024]{1,0:T(8,128)(2,1)S(1)} %bitcast.9, f32[512,8]{1,0:T(8,128)S(1)} %copy-done.6), custom_call_target="tpu_custom_call" | custom-call | flops 1073741824 | bytes 4194304 | tf_op jit(solution)/shard_map/order/order_rows/pallas_call | solution.py:393
  (20 shorter events, 0.1 us)
Async XLA Ops:
  3.2 27.8 %collective-permute-start = (bf16[64,4096]{1,0:T(8,128)(2,1)}, bf16[64,4096]{1,0:T(8,128)(2,1)S(1)}, u32[]{:S(2)}, u32[]{:S(2)}) collective-permute-start(bf16[64,4096]{1,0:T(8,128)(2,1)} %prepare_bank.1.refs_0_), channel_id=1, source_target_pairs={{0,56},{4,60},{8,0},{12,4},{16,8},{20,12},{24,16},{28,20},{32,24},... | collective-permute-start | bytes 1572872 | tf_op jit(solution)/shard_map/ring/ppermute | solution.py:431
  9.6 21.4 %collective-permute-start.1 = (bf16[64,4096]{1,0:T(8,128)(2,1)}, bf16[64,4096]{1,0:T(8,128)(2,1)S(1)}, u32[]{:S(2)}, u32[]{:S(2)}) collective-permute-start(bf16[64,4096]{1,0:T(8,128)(2,1)} %prepare_bank.1.refs_0_), channel_id=1, source_target_pairs={{0,8},{4,12},{8,16},{12,20},{16,24},{20,28},{24,32},{28,36},{32,40... | collective-permute-start | bytes 1572872 | tf_op jit(solution)/shard_map/ring/ppermute | solution.py:430
  11.8 19.2 %all-to-all-start = ((f32[32,1,4224]{2,1,0:T(1,128)}), f32[32,1,4224]{2,1,0:T(1,128)S(1)}, u32[]{:S(2)}, u32[]{:S(2)}) async-start(f32[32,1,4224]{2,1,0:T(1,128)} %get-tuple-element.22), calls=%async_computation | async-start | bytes 1081344 | tf_op jit(solution)/shard_map/exchange/all_to_all | solution.py:439
  19.8 2.2 %copy-start.4 = (bf16[16,256,512]{2,1,0:T(8,128)(2,1)S(1)}, bf16[16,256,512]{2,1,0:T(8,128)(2,1)}, u32[]{:S(2)}) copy-start(bf16[16,256,512]{2,1,0:T(8,128)(2,1)} %constant.2.clone.source) | copy-start | bytes 12582916
  22.0 11.9 %copy-start.9 = (f32[2,4]{1,0:T(2,128)S(1)}, f32[2,4]{1,0:T(2,128)}, u32[]{:S(2)}) copy-start(f32[2,4]{1,0:T(2,128)} %antenna_ref.1) | copy-start | bytes 100
  22.0 12.6 %copy-start.5 = (bf16[64,4096]{1,0:T(8,128)(2,1)S(1)}, bf16[64,4096]{1,0:T(8,128)(2,1)}, u32[]{:S(2)}) copy-start(bf16[64,4096]{1,0:T(8,128)(2,1)} %prepare_bank.1.refs_0_) | copy-start | bytes 1572868
  22.0 12.6 %copy-start.6 = (f32[512,8]{1,0:T(8,128)S(1)}, f32[512,8]{1,0:T(8,128)}, u32[]{:S(2)}) copy-start(f32[512,8]{1,0:T(8,128)} %get-tuple-element.29.refs_5_.refs_2_) | copy-start | bytes 49156
  22.3 1.9 %copy-start = (bf16[16,256,512]{2,1,0:T(8,128)(2,1)}, bf16[16,256,512]{2,1,0:T(8,128)(2,1)S(1)}, u32[]{:S(2)}) copy-start(bf16[16,256,512]{2,1,0:T(8,128)(2,1)S(1)} %stage_basis.1.refs_4_.refs_3_) | copy-start | bytes 12582916
  31.0 18.1 %collective-permute-start.2 = (bf16[64,4096]{1,0:T(8,128)(2,1)S(1)}, bf16[64,4096]{1,0:T(8,128)(2,1)S(1)}, u32[]{:S(2)}, u32[]{:S(2)}) collective-permute-start(bf16[64,4096]{1,0:T(8,128)(2,1)S(1)} %collective-permute-done.refs_2_), channel_id=1, source_target_pairs={{0,56},{4,60},{8,0},{12,4},{16,8},{20,12},{24,16},{28,20},{32,24},... | collective-permute-start | bytes 1572872 | tf_op jit(solution)/shard_map/ring/ppermute | solution.py:431
  34.0 15.2 %collective-permute-start.3 = (bf16[64,4096]{1,0:T(8,128)(2,1)S(1)}, bf16[64,4096]{1,0:T(8,128)(2,1)S(1)}, u32[]{:S(2)}, u32[]{:S(2)}) collective-permute-start(bf16[64,4096]{1,0:T(8,128)(2,1)S(1)} %collective-permute-done.1.refs_1_), channel_id=1, source_target_pairs={{0,8},{4,12},{8,16},{12,20},{16,24},{20,28},{24,32},{28,36},{32,40... | collective-permute-start | bytes 1572872 | tf_op jit(solution)/shard_map/ring/ppermute | solution.py:430
  34.6 2.2 %copy-start.1 = (bf16[16,256,512]{2,1,0:T(8,128)(2,1)S(1)}, bf16[16,256,512]{2,1,0:T(8,128)(2,1)}, u32[]{:S(2)}) copy-start(bf16[16,256,512]{2,1,0:T(8,128)(2,1)} %copy-done) | copy-start | bytes 12582916
  36.8 15.1 %copy-start.2 = (bf16[16,256,512]{2,1,0:T(8,128)(2,1)S(1)}, bf16[16,256,512]{2,1,0:T(8,128)(2,1)}, u32[]{:S(2)}) copy-start(bf16[16,256,512]{2,1,0:T(8,128)(2,1)} %copy-done) | copy-start | bytes 12582916
  49.1 12.4 %collective-permute-start.4 = (bf16[64,4096]{1,0:T(8,128)(2,1)S(1)}, bf16[64,4096]{1,0:T(8,128)(2,1)S(1)}, u32[]{:S(2)}, u32[]{:S(2)}) collective-permute-start(bf16[64,4096]{1,0:T(8,128)(2,1)S(1)} %collective-permute-done.2.refs_1_), channel_id=1, source_target_pairs={{0,56},{4,60},{8,0},{12,4},{16,8},{20,12},{24,16},{28,20},{32,24},... | collective-permute-start | bytes 1572872 | tf_op jit(solution)/shard_map/ring/ppermute | solution.py:431
  51.9 12.8 %collective-permute-start.5 = (bf16[64,4096]{1,0:T(8,128)(2,1)S(1)}, bf16[64,4096]{1,0:T(8,128)(2,1)S(1)}, u32[]{:S(2)}, u32[]{:S(2)}) collective-permute-start(bf16[64,4096]{1,0:T(8,128)(2,1)S(1)} %collective-permute-done.3.refs_0_), channel_id=1, source_target_pairs={{0,8},{4,12},{8,16},{12,20},{16,24},{20,28},{24,32},{28,36},{32,40... | collective-permute-start | bytes 1572872 | tf_op jit(solution)/shard_map/ring/ppermute | solution.py:430
  64.7 0.8 copy-start.7
  65.5 9.8 %collective-permute-start.6 = (bf16[32,4096]{1,0:T(8,128)(2,1)S(1)}, bf16[32,4096]{1,0:T(8,128)(2,1)S(1)}, u32[]{:S(2)}, u32[]{:S(2)}) collective-permute-start(bf16[32,4096]{1,0:T(8,128)(2,1)S(1)} %slice.6), channel_id=1, source_target_pairs={{0,8},{4,12},{8,16},{12,20},{16,24},{20,28},{24,32},{28,36},{32,40... | collective-permute-start | bytes 786440 | tf_op jit(solution)/shard_map/ring/ppermute | solution.py:434
  65.5 9.7 %collective-permute-start.7 = (bf16[32,4096]{1,0:T(8,128)(2,1)S(1)}, bf16[32,4096]{1,0:T(8,128)(2,1)S(1)}, u32[]{:S(2)}, u32[]{:S(2)}) collective-permute-start(bf16[32,4096]{1,0:T(8,128)(2,1)S(1)} %slice.7), channel_id=1, source_target_pairs={{0,56},{4,60},{8,0},{12,4},{16,8},{20,12},{24,16},{28,20},{32,24},... | collective-permute-start | bytes 786440 | tf_op jit(solution)/shard_map/ring/ppermute | solution.py:434
  68.4 24.7 %all-to-all-start.1 = ((bf16[8,80,1024]{2,1,0:T(8,128)(2,1)}), bf16[8,80,1024]{2,1,0:T(8,128)(2,1)S(1)}, u32[]{:S(2)}, u32[]{:S(2)}) async-start(bf16[8,80,1024]{2,1,0:T(8,128)(2,1)} %bitcast.3), calls=%async_computation.1 | async-start | bytes 2621440 | tf_op jit(solution)/shard_map/back/all_to_all | solution.py:463
  75.3 2.2 %copy-start.3 = (bf16[16,256,512]{2,1,0:T(8,128)(2,1)S(1)}, bf16[16,256,512]{2,1,0:T(8,128)(2,1)}, u32[]{:S(2)}) copy-start(bf16[16,256,512]{2,1,0:T(8,128)(2,1)} %copy-done) | copy-start | bytes 12582916
  77.5 1.0 copy-start.8
where the time goes:
time: 112 us
  Pallas kernels  41.3 us (37%)
  starting transfers between devices  29.9 us (27%)
  blocking collectives  15.5 us (14%)
  waiting for transfers between devices  14.6 us (13%)
  local copies, waits for them, and re-layouts  10.4 us (9%)
    pallas_call x3, Pallas kernels, filter_banks(): pl.pallas_call(functools.partial(filter_kernel, count, first, slot), out_...  31.8 us
    all_to_all x1, blocking collectives, per_device(): lax.all_to_all(rows.reshape(PEERS, m * CAP, STEP), 'seg', split_axis=0, c...  15.5 us
    ppermute x3, starting transfers between devices, ring(): held[k] = lax.ppermute(held[k - 1], 'seg', down)  12.1 us
    unnamed x20, local copies, waits for them, and re-layouts  10.3 us
    all_to_all x1, starting transfers between devices, per_device(): lax.all_to_all(packet, ('seg', 'det'), split_axis=0, concat_axis=0, tiled...  8.04 us
    all_to_all x1, starting transfers between devices, per_device(): lax.all_to_all(rows.reshape(PEERS, m * CAP, STEP), 'seg', split_axis=0, c...  6.81 us
    all_to_all x1, waiting for transfers between devices, per_device(): lax.all_to_all(packet, ('seg', 'det'), split_axis=0, concat_axis=0, tiled...  6.73 us
    pallas_call x1, Pallas kernels, order_rows(): pl.pallas_call(functools.partial(order_kernel, [r.shape[0] for r in rows]...  3.27 us
  transfers between devices with their start and end apart: 10, of which 4 were waited for; matrix products, arithmetic and copies ran while one was open for 0% of the time, Pallas kernels for 31%

commit v1 on v0

--- a/solution.py
+++ b/solution.py
@@ -83,7 +83,7 @@
     want = (slot_ref[...] + 1).astype(jnp.float32)
     size = lookup(dz, [len(PARTS[g]) * CAP for g in part_of])
     place = (start * PEERS + peer * size + rank).astype(jnp.float32)
-    place_ref[...] = jnp.transpose(jnp.broadcast_to(place, (8, n)))
+    place_ref[...] = jnp.broadcast_to(place, (8, n))
     wanted = jnp.where(peer == lax.broadcasted_iota(jnp.int32, (PEERS, n), 0), want, 0.0)
     spot = (start + rank) == lax.broadcasted_iota(jnp.int32, (NZ * CAP, n), 0)
     table = (
@@ -147,7 +147,7 @@
         head_kernel,
         out_shape=[
             jax.ShapeDtypeStruct((PEERS * ND, 1, WIDE + 128), jnp.float32),
-            jax.ShapeDtypeStruct((n, 8), jnp.float32),
+            jax.ShapeDtypeStruct((8, n), jnp.float32),
         ],
         in_specs=[smem] + [vmem] * 3,
         out_specs=[vmem] * 2,
@@ -165,7 +165,7 @@
         in_specs=[pl.BlockSpec(memory_space=pltpu.SMEM), vmem],
         out_specs=vmem,
         compiler_params=pltpu.CompilerParams(vmem_limit_bytes=58 << 20),
-        cost_estimate=pl.CostEstimate(flops=4 << 20, bytes_accessed=2 << 20, transcendentals=0),
+        cost_estimate=pl.CostEstimate(flops=8 << 30, bytes_accessed=2 << 20, transcendentals=0),
         name="prepare_bank",
     )(dur, bank)
 
@@ -206,6 +206,11 @@
         return -re, -im
     if k == 12:
         return im, -re
+    r = math.sqrt(0.5)
+    if k == 2:
+        return (re - im) * r, (re + im) * r
+    if k == 6:
+        return (re + im) * -r, (re - im) * r
     c, s = math.cos(math.pi * k / 8), math.sin(math.pi * k / 8)
     return re * c - im * s, re * s + im * c
 
@@ -252,9 +257,9 @@
     )(basis)
 
 
-def filter_kernel(count, first, slot, *refs):
+def filter_kernel(count, first, slot, spread, *refs):
     banks = refs[:count]
-    packet_ref, basis_ref, _, whole_ref, token_ref, bank, column, coh, spec, xs, norms, out_ref, bank_sems, out_sem = refs[count:]
+    packet_ref, basis_ref, _, *outs, token_ref, bank, column, coh, spec, xs, norms, out_ref, bank_sems, out_sem = refs[count:]
     half = PEERS * CAP
     loads = [pltpu.make_async_copy(banks[i], bank.at[i], bank_sems.at[i]) for i in range(count)]
     for load in loads:
@@ -335,25 +340,38 @@
         return 0
 
     lax.fori_loop(0, count, block, 0)
-    put = pltpu.make_async_copy(out_ref, whole_ref.at[:, pl.ds(slot, count)], out_sem)
-    put.start()
+    if spread:
+        x, c = lax.axis_index("seg") // (NZ * NC), lax.axis_index("seg") % NC
+        puts = [
+            pltpu.make_async_copy(
+                out_ref.at[((x + dx) % NX) * NC + (c + dc) % NC], outs[dx * NC + dc], out_sem.at[dx * NC + dc]
+            )
+            for dx in range(NX)
+            for dc in range(NC)
+        ]
+    else:
+        puts = [pltpu.make_async_copy(out_ref, outs[0].at[:, pl.ds(slot, count)], out_sem.at[0])]
+    for put in puts:
+        put.start()
     token_ref[...] = norms[0:8, :]
-    put.wait()
-
-
-def filter_banks(banks, first, packet, basis, slot, total, before):
+    for put in puts:
+        put.wait()
+
+
+def filter_banks(banks, first, packet, basis, slot, total, before, spread=False):
     count = len(banks)
     vmem = pl.BlockSpec(memory_space=pltpu.VMEM)
     any_space = pl.BlockSpec(memory_space=pl.ANY)
     half = PEERS * CAP
     return pl.pallas_call(
-        functools.partial(filter_kernel, count, first, slot),
+        functools.partial(filter_kernel, count, first, slot, spread),
         out_shape=[
-            jax.ShapeDtypeStruct((PEERS, total, CAP, STEP), jnp.bfloat16),
-            jax.ShapeDtypeStruct((8, 128), jnp.float32),
-        ],
+            jax.ShapeDtypeStruct(shape, jnp.bfloat16)
+            for shape in ([(count, CAP, STEP)] * PEERS if spread else [(PEERS, total, CAP, STEP)])
+        ]
+        + [jax.ShapeDtypeStruct((8, 128), jnp.float32)],
         in_specs=[any_space] * count + [vmem, vmem, any_space],
-        out_specs=[any_space, vmem],
+        out_specs=[any_space] * (PEERS if spread else 1) + [vmem],
         input_output_aliases={count + 2: 0} if slot else {},
         scratch_shapes=[
             pltpu.VMEM((count, SLOTS, WIDE), jnp.bfloat16),
@@ -364,43 +382,56 @@
             pltpu.VMEM((half, 128), jnp.float32),
             pltpu.VMEM((PEERS, count, CAP, STEP), jnp.bfloat16),
             pltpu.SemaphoreType.DMA((count,)),
-            pltpu.SemaphoreType.DMA,
+            pltpu.SemaphoreType.DMA((PEERS,)),
         ],
         compiler_params=pltpu.CompilerParams(vmem_limit_bytes=24 << 20),
         cost_estimate=pl.CostEstimate(
-            flops=count * (3 << 30), bytes_accessed=(5 << 20) + count * (1 << 20), transcendentals=0
+            flops=0 if spread else count * (3 << 30), bytes_accessed=1 << 20, transcendentals=0
         ),
         name=f"filter{count}_{first}",
     )(*banks, packet, basis, before)
 
 
-def order_kernel(sizes, *refs):
-    rows = refs[: len(sizes)]
-    place_ref, out_ref = refs[len(sizes) :]
+def order_kernel(near_ref, *refs):
+    *pieces, place_ref, out_ref, far = refs
+    count = pieces[0].shape[0]
+    x, c = lax.axis_index("seg") // (NZ * NC), lax.axis_index("seg") % NC
+
+    @pl.when(pl.program_id(0) == 0)
+    def _():
+        for dx in range(NX):
+            for dc in range(NC):
+                peer = ((x + NX - dx) % NX) * NC + (c + dc) % NC
+                rows = pl.ds(pl.multiple_of(peer * count, CAP), count)
+                far[rows, :] = pieces[dx * NC + dc][...]
+
+    column = jnp.transpose(place_ref[...])[:, 0:1]
     out, first = None, 0
-    for n, ref in zip(sizes, rows):
-        lane = first + lax.broadcasted_iota(jnp.int32, (place_ref.shape[0], n), 1)
-        pick = (place_ref[:, 0:1] == lane.astype(jnp.float32)).astype(jnp.bfloat16)
+    for ref in (near_ref, far):
+        n = ref.shape[0]
+        lane = (first + lax.broadcasted_iota(jnp.int32, (column.shape[0], n), 1)).astype(jnp.float32)
+        pick = (column == lane).astype(jnp.bfloat16)
         part = jnp.dot(pick, ref[...], preferred_element_type=jnp.float32)
         out = part if out is None else out + part
         first += n
     out_ref[...] = jnp.where(out < 0.0, jnp.nan, out)
 
 
-def order_rows(rows, place):
-    n = place.shape[0]
+def order_rows(near, pieces, place):
+    n = place.shape[1]
     step = 128
+    whole = [pl.BlockSpec(r.shape, lambda i: (0, 0)) for r in [near, *pieces]]
     return pl.pallas_call(
-        functools.partial(order_kernel, [r.shape[0] for r in rows]),
+        order_kernel,
         out_shape=jax.ShapeDtypeStruct((n, STEP), jnp.float32),
         grid=(n // step,),
-        in_specs=[pl.BlockSpec(r.shape, lambda i: (0, 0)) for r in rows]
-        + [pl.BlockSpec((step, 8), lambda i: (i, 0))],
+        in_specs=whole + [pl.BlockSpec((8, step), lambda i: (0, i))],
         out_specs=pl.BlockSpec((step, STEP), lambda i: (i, 0)),
+        scratch_shapes=[pltpu.VMEM((PEERS * pieces[0].shape[0], STEP), jnp.bfloat16)],
         compiler_params=pltpu.CompilerParams(vmem_limit_bytes=24 << 20),
         cost_estimate=pl.CostEstimate(flops=1 << 30, bytes_accessed=4 << 20, transcendentals=0),
         name="order_rows",
-    )(*rows, place)
+    )(near, *pieces, place)
 
 
 def per_device(basis, strain, antenna, delays, template_bank, duration_bin, owner_seg, slot_index):
@@ -416,11 +447,13 @@
     half = SLOTS // 2
 
     with jax.named_scope("head"):
-        own = prepare_bank(duration_bin, template_bank[0])
-        own, strain = lax.optimization_barrier((own, strain))
         packet, place = head(
             delays, strain.reshape(WIDE // 128, 128), owner_seg.reshape(1, -1), slot_index
         )
+
+    packet, template_bank = lax.optimization_barrier((packet, template_bank))
+    with jax.named_scope("bank"):
+        own = prepare_bank(duration_bin, template_bank[0])
 
     held = {0: own}
 
@@ -441,36 +474,43 @@
         )
         packet, held[1], held[-1] = lax.optimization_barrier((packet, held[1], held[-1]))
         packet = combine(antenna, packet)
-        basis = stage(basis)
     ring(2)
 
-    back, first, token = [], 0, place
-    for part in PARTS:
-        m = len(part)
-        rows, slot = token, 0
-        for step in CALLS[part]:
-            with jax.named_scope("filter"):
-                rows, token = filter_banks(
-                    [held[d] for d in step], first + slot * CAP, packet, basis, slot, m, rows
-                )
-            slot += len(step)
-            k = max(held)
-            if k < 4:
-                token, held[k], held[-k] = lax.optimization_barrier((token, held[k], held[-k]))
-                ring(k + 1)
-        first += m * CAP
-        with jax.named_scope("back"):
-            rows = lax.all_to_all(
-                rows.reshape(PEERS, m * CAP, STEP),
-                "seg",
-                split_axis=0,
-                concat_axis=0,
-                tiled=True,
-                axis_index_groups=back_groups,
+    near_part, far_part = PARTS
+    rows, slot, token = place, 0, place
+    for step in CALLS[near_part]:
+        with jax.named_scope("filter"):
+            rows, token = filter_banks(
+                [held[d] for d in step], slot * CAP, packet, basis, slot, len(near_part), rows
             )
-        back.append(rows.reshape(PEERS * m * CAP, STEP))
+        slot += len(step)
+        k = max(held)
+        token, held[k], held[-k] = lax.optimization_barrier((token, held[k], held[-k]))
+        ring(k + 1)
+    with jax.named_scope("back"):
+        near = lax.all_to_all(
+            rows.reshape(PEERS, slot * CAP, STEP),
+            "seg",
+            split_axis=0,
+            concat_axis=0,
+            tiled=True,
+            axis_index_groups=back_groups,
+        )
+    m = len(far_part)
+    token, late_basis = lax.optimization_barrier((token, basis))
+    late_basis = stage(late_basis)
+    with jax.named_scope("filter"):
+        *pieces, token = filter_banks(
+            [held[d] for d in far_part], slot * CAP, packet, late_basis, 0, m, token, spread=True
+        )
+    with jax.named_scope("back"):
+        for k in range(1, PEERS):
+            dx, dc = divmod(k, NC)
+            to = [(at(x, z, c), at((x + dx) % NX, z, (c + dc) % NC)) for x, z, c in places]
+            pieces[k] = lax.ppermute(pieces[k], "seg", to)
     with jax.named_scope("order"):
-        return order_rows(back, place)[None]
+        near = near.reshape(PEERS * slot * CAP, STEP)
+        return order_rows(near, [p.reshape(m * CAP, STEP) for p in pieces], place)[None]
 
 
 def solution(mesh):

time: 112 us -> 106 us (0.946)
  local copies, waits for them, and re-layouts: 10.4 us -> 3.28 us
  blocking collectives: 15.5 us -> 19 us
  Pallas kernels: 41.3 us -> 43.6 us
  waiting for transfers between devices: 14.6 us -> 12.3 us
  starting transfers between devices: 29.9 us -> 27.7 us
    all_to_all x2 -> x1, waiting for transfers between devices: 9.89 us -> 0.01 us  [per_device(): lax.all_to_all(rows.reshape(PEERS, slot * CAP, STEP), 'seg', split_axis=0...]
    ppermute x0 -> x7, starting transfers between devices: none -> 9.57 us  [per_device(): pieces[k] = lax.ppermute(pieces[k], 'seg', to)]
    all_to_all x2 -> x1, starting transfers between devices: 14.8 us -> 5.56 us  [per_device(): lax.all_to_all(rows.reshape(PEERS, slot * CAP, STEP), 'seg', split_axis=0...]
    unnamed x20 -> x12, local copies, waits for them, and re-layouts: 10.3 us -> 3.24 us
    ppermute x0 -> x7, waiting for transfers between devices: none -> 6.16 us  [per_device(): pieces[k] = lax.ppermute(pieces[k], 'seg', to)]
    ppermute x1, waiting for transfers between devices: 0.01 us -> 3.82 us  [ring(): lax.ppermute(held[3][half:], 'seg', down)]
    ppermute x3, starting transfers between devices: 12.1 us -> 8.42 us  [ring(): held[k] = lax.ppermute(held[k - 1], 'seg', down)]
    all_to_all x1, blocking collectives: 15.5 us -> 19 us  [per_device(): lax.all_to_all(packet, ('seg', 'det'), split_axis=0, concat_axis=0, tiled...]
  transfers between devices with their start and end apart: 10 -> 16, of which waited for: 4 -> 5; matrix products, arithmetic and copies ran while one was open for 0% -> 0% of each run, Pallas kernels for 31% -> 33%
where the time goes in v1:
time: 106 us
  Pallas kernels  43.6 us (41%)
  starting transfers between devices  27.7 us (26%)
  blocking collectives  19 us (18%)
  waiting for transfers between devices  12.3 us (12%)
  local copies, waits for them, and re-layouts  3.28 us (3%)
    pallas_call x3, Pallas kernels, filter_banks(): pl.pallas_call(functools.partial(filter_kernel, count, first, slot, sprea...  33.6 us
    all_to_all x1, blocking collectives, per_device(): lax.all_to_all(packet, ('seg', 'det'), split_axis=0, concat_axis=0, tiled...  19 us
    ppermute x7, starting transfers between devices, per_device(): pieces[k] = lax.ppermute(pieces[k], 'seg', to)  9.57 us
    ppermute x3, starting transfers between devices, ring(): held[k] = lax.ppermute(held[k - 1], 'seg', down)  8.42 us
    ppermute x7, waiting for transfers between devices, per_device(): pieces[k] = lax.ppermute(pieces[k], 'seg', to)  6.16 us
    all_to_all x1, starting transfers between devices, per_device(): lax.all_to_all(rows.reshape(PEERS, slot * CAP, STEP), 'seg', split_axis=0...  5.56 us
    ppermute x1, waiting for transfers between devices, ring(): lax.ppermute(held[3][half:], 'seg', down)  3.82 us
    pallas_call x1, Pallas kernels, order_rows(): pl.pallas_call(order_kernel, out_shape=jax.ShapeDtypeStruct((n, STEP), jn...  3.58 us
  transfers between devices with their start and end apart: 16, of which 5 were waited for; matrix products, arithmetic and copies ran while one was open for 0% of the time, Pallas kernels for 33%

profile of v1, /device:TPU:1, one launch (start us, length us, event | category | flops | bytes accessed | tf_op | source)
XLA Modules:
  0.0 106.0 jit_solution(881723284963341592)
XLA Ops:
  0.0 2.1 %head.1 = (f32[32,1,4224]{2,1,0:T(1,128)}, f32[8,512]{1,0:T(8,128)}) custom-call(s32[4]{0:T(128)} %delays_ref.1, f32[32,128]{1,0:T(8,128)} %bitcast.23, s32[1,512]{1,0:T(1,128)} %bitcast.24, s32[1,512]{1,0:T(1,128)} %slot_ref.1), custom_call_target="tpu_custom_call" | custom-call | flops 4194304 | bytes 2097152 | tf_op jit(solution)/shard_map/head/head/pallas_call | solution.py:146
  2.1 3.4 %prepare_bank.1.refs_0_ = bf16[64,4096]{1,0:T(8,128)(2,1)} custom-call(s32[1,64]{1,0:T(1,128)} %dur_ref.1, bf16[64,4096]{1,0:T(8,128)(2,1)} %bitcast.25), custom_call_target="tpu_custom_call" | custom-call | flops 8589934592 | bytes 2097152 | tf_op jit(solution)/shard_map/bank/prepare_bank/pallas_call | solution.py:162
  5.5 2.5 %collective-permute-start.1 = (bf16[64,4096]{1,0:T(8,128)(2,1)}, bf16[64,4096]{1,0:T(8,128)(2,1)S(1)}, u32[]{:S(2)}, u32[]{:S(2)}) collective-permute-start(bf16[64,4096]{1,0:T(8,128)(2,1)} %prepare_bank.1.refs_0_), channel_id=1, source_target_pairs={{0,8},{4,12},{8,16},{12,20},{16,24},{20,28},{24,32},{28,36},{32,40... | collective-permute-start | bytes 1572872 | tf_op jit(solution)/shard_map/ring/ppermute | solution.py:463
  8.0 3.9 %collective-permute-start = (bf16[64,4096]{1,0:T(8,128)(2,1)}, bf16[64,4096]{1,0:T(8,128)(2,1)S(1)}, u32[]{:S(2)}, u32[]{:S(2)}) collective-permute-start(bf16[64,4096]{1,0:T(8,128)(2,1)} %prepare_bank.1.refs_0_), channel_id=1, source_target_pairs={{0,56},{4,60},{8,0},{12,4},{16,8},{20,12},{24,16},{28,20},{32,24},... | collective-permute-start | bytes 1572872 | tf_op jit(solution)/shard_map/ring/ppermute | solution.py:464
  11.9 19.0 %all_to_all.10.packet_ref = f32[32,1,4224]{2,1,0:T(1,128)S(1)} all-to-all(f32[32,1,4224]{2,1,0:T(1,128)S(1)} %copy-done.5), channel_id=1, replica_groups={{0,1,2,3,4,5,6,7,64,65,66,67,68,69,70,71,128,129,130,131,132,133,134,13..., dimensions={0} | all-to-all | bytes 1081344 | tf_op jit(solution)/shard_map/exchange/all_to_all | solution.py:472
  30.9 0.0 collective-permute-done.1.refs_1_
  30.9 1.7 %collective-permute-start.2 = (bf16[64,4096]{1,0:T(8,128)(2,1)S(1)}, bf16[64,4096]{1,0:T(8,128)(2,1)S(1)}, u32[]{:S(2)}, u32[]{:S(2)}) collective-permute-start(bf16[64,4096]{1,0:T(8,128)(2,1)S(1)} %collective-permute-done.refs_2_), channel_id=1, source_target_pairs={{0,56},{4,60},{8,0},{12,4},{16,8},{20,12},{24,16},{28,20},{32,24},... | collective-permute-start | bytes 1572872 | tf_op jit(solution)/shard_map/ring/ppermute | solution.py:464
  32.7 0.6 combine.1.refs_3_.refs_2_
  33.3 1.0 copy-done.4
  34.3 12.3 %filter3_0.1 = (bf16[8,5,16,1024]{3,2,1,0:T(8,128)(2,1)}, f32[8,128]{1,0:T(8,128)}) custom-call(bf16[64,4096]{1,0:T(8,128)(2,1)S(1)} %copy-done.4, bf16[64,4096]{1,0:T(8,128)(2,1)S(1)} %collective-permute-done.1.refs_1_, bf16[64,4096]{1,0:T(8,128)(2,1)S(1)} %collective-permute-done.refs_2_, f32[8,1,8320]{2,1,0:T(1,128)S(1)} %combine.1.refs_3_.refs_2_, ...), custom_call_target="tpu_custom_call" | custom-call | flops 9663676416 | bytes 1048576 | tf_op jit(solution)/shard_map/filter/filter3_0/pallas_call | solution.py:366
  46.6 0.1 collective-permute-start.5
  46.7 2.7 %collective-permute-start.4 = (bf16[64,4096]{1,0:T(8,128)(2,1)S(1)}, bf16[64,4096]{1,0:T(8,128)(2,1)S(1)}, u32[]{:S(2)}, u32[]{:S(2)}) collective-permute-start(bf16[64,4096]{1,0:T(8,128)(2,1)S(1)} %collective-permute-done.2.refs_1_), channel_id=1, source_target_pairs={{0,56},{4,60},{8,0},{12,4},{16,8},{20,12},{24,16},{28,20},{32,24},... | collective-permute-start | bytes 1572872 | tf_op jit(solution)/shard_map/ring/ppermute | solution.py:464
  49.5 8.9 %filter2_48.1 = (bf16[8,5,16,1024]{3,2,1,0:T(8,128)(2,1)}, f32[8,128]{1,0:T(8,128)S(1)}) custom-call(bf16[64,4096]{1,0:T(8,128)(2,1)} %collective-permute-done.3.refs_0_, bf16[64,4096]{1,0:T(8,128)(2,1)S(1)} %collective-permute-done.2.refs_1_, f32[8,1,8320]{2,1,0:T(1,128)S(1)} %combine.1.refs_3_.refs_2_, ...), custom_call_target="tpu_custom_call", output_to_operand_aliasing={{0}: (4, {})} | custom-call | flops 6442450944 | bytes 1048576 | tf_op jit(solution)/shard_map/filter/filter2_48/pallas_call | solution.py:366
  58.4 5.6 %all-to-all-start.1 = ((bf16[8,80,1024]{2,1,0:T(8,128)(2,1)}), bf16[8,80,1024]{2,1,0:T(8,128)(2,1)S(1)}, u32[]{:S(2)}, u32[]{:S(2)}) async-start(bf16[8,80,1024]{2,1,0:T(8,128)(2,1)} %bitcast.3), calls=%async_computation.1 | async-start | bytes 2621440 | tf_op jit(solution)/shard_map/back/all_to_all | solution.py:491
  64.0 1.5 %collective-permute-start.7 = (bf16[32,4096]{1,0:T(8,128)(2,1)S(1)}, bf16[32,4096]{1,0:T(8,128)(2,1)S(1)}, u32[]{:S(2)}, u32[]{:S(2)}) collective-permute-start(bf16[32,4096]{1,0:T(8,128)(2,1)S(1)} %slice.7), channel_id=1, source_target_pairs={{0,56},{4,60},{8,0},{12,4},{16,8},{20,12},{24,16},{28,20},{32,24},... | collective-permute-start | bytes 786440 | tf_op jit(solution)/shard_map/ring/ppermute | solution.py:467
  65.5 0.0 collective-permute-start.6
  65.5 2.2 %copy-done.1 = bf16[16,256,512]{2,1,0:T(8,128)(2,1)S(1)} copy-done((bf16[16,256,512]{2,1,0:T(8,128)(2,1)S(1)}, bf16[16,256,512]{2,1,0:T(8,128)(2,1)}, u32[]{:S(2)}) %copy-start.1) | copy-done | bytes 4194328
  67.7 0.3 stage_basis.1.refs_4_
  68.0 3.8 %collective-permute-done.7 = bf16[32,4096]{1,0:T(8,128)(2,1)S(1)} collective-permute-done((bf16[32,4096]{1,0:T(8,128)(2,1)S(1)}, bf16[32,4096]{1,0:T(8,128)(2,1)S(1)}, u32[]{:S(2)}, u32[]{:S(2)}) %collective-permute-start.7) | collective-permute-done | bytes 262176 | tf_op jit(solution)/shard_map/ring/ppermute | solution.py:467
  71.8 2.3 %collective-permute-done.6 = bf16[32,4096]{1,0:T(8,128)(2,1)S(1)} collective-permute-done((bf16[32,4096]{1,0:T(8,128)(2,1)S(1)}, bf16[32,4096]{1,0:T(8,128)(2,1)S(1)}, u32[]{:S(2)}, u32[]{:S(2)}) %collective-permute-start.6) | collective-permute-done | bytes 262176 | tf_op jit(solution)/shard_map/ring/ppermute | solution.py:467
  74.2 12.4 %filter3_80.1 = (bf16[3,16,1024]{2,1,0:T(8,128)(2,1)S(1)}, bf16[3,16,1024]{2,1,0:T(8,128)(2,1)S(1)}, bf16[3,16,1024]{2,1,0:T(8,128)(2,1)S(1)}, bf16[3,16,1024]{2...) custom-call(bf16[64,4096]{1,0:T(8,128)(2,1)S(1)} %collective-permute, ...), custom_call_target="tpu_custom_call" | custom-call | bytes 1048576 | tf_op jit(solution)/shard_map/filter/filter3_80/pallas_call | solution.py:366
  86.6 1.4 %collective-permute-start.8 = (bf16[3,16,1024]{2,1,0:T(8,128)(2,1)S(1)}, bf16[3,16,1024]{2,1,0:T(8,128)(2,1)S(1)}, u32[]{:S(2)}, u32[]{:S(2)}) collective-permute-start(bf16[3,16,1024]{2,1,0:T(8,128)(2,1)S(1)} %get-tuple-element.48), channel_id=1, source_target_pairs={{0,4},{4,0},{8,12},{12,8},{16,20},{20,16},{24,28},{28,24},{32,36},... | collective-permute-start | bytes 294920 | tf_op jit(solution)/shard_map/back/ppermute | solution.py:510
  88.0 1.4 %collective-permute-start.9 = (bf16[3,16,1024]{2,1,0:T(8,128)(2,1)S(1)}, bf16[3,16,1024]{2,1,0:T(8,128)(2,1)S(1)}, u32[]{:S(2)}, u32[]{:S(2)}) collective-permute-start(bf16[3,16,1024]{2,1,0:T(8,128)(2,1)S(1)} %get-tuple-element.49), channel_id=1, source_target_pairs={{0,64},{4,68},{8,72},{12,76},{16,80},{20,84},{24,88},{28,92},{32,9... | collective-permute-start | bytes 294920 | tf_op jit(solution)/shard_map/back/ppermute | solution.py:510
  89.4 1.4 %collective-permute-start.10 = (bf16[3,16,1024]{2,1,0:T(8,128)(2,1)S(1)}, bf16[3,16,1024]{2,1,0:T(8,128)(2,1)S(1)}, u32[]{:S(2)}, u32[]{:S(2)}) collective-permute-start(bf16[3,16,1024]{2,1,0:T(8,128)(2,1)S(1)} %get-tuple-element.50), channel_id=1, source_target_pairs={{0,68},{4,64},{8,76},{12,72},{16,84},{20,80},{24,92},{28,88},{32,1... | collective-permute-start | bytes 294920 | tf_op jit(solution)/shard_map/back/ppermute | solution.py:510
  90.8 1.3 %collective-permute-start.11 = (bf16[3,16,1024]{2,1,0:T(8,128)(2,1)S(1)}, bf16[3,16,1024]{2,1,0:T(8,128)(2,1)S(1)}, u32[]{:S(2)}, u32[]{:S(2)}) collective-permute-start(bf16[3,16,1024]{2,1,0:T(8,128)(2,1)S(1)} %get-tuple-element.51), channel_id=1, source_target_pairs={{0,128},{4,132},{8,136},{12,140},{16,144},{20,148},{24,152},{28,15... | collective-permute-start | bytes 294920 | tf_op jit(solution)/shard_map/back/ppermute | solution.py:510
  92.1 2.0 %collective-permute-start.12 = (bf16[3,16,1024]{2,1,0:T(8,128)(2,1)S(1)}, bf16[3,16,1024]{2,1,0:T(8,128)(2,1)S(1)}, u32[]{:S(2)}, u32[]{:S(2)}) collective-permute-start(bf16[3,16,1024]{2,1,0:T(8,128)(2,1)S(1)} %get-tuple-element.52), channel_id=1, source_target_pairs={{0,132},{4,128},{8,140},{12,136},{16,148},{20,144},{24,156},{28,15... | collective-permute-start | bytes 294920 | tf_op jit(solution)/shard_map/back/ppermute | solution.py:510
  94.2 1.5 %collective-permute-start.13 = (bf16[3,16,1024]{2,1,0:T(8,128)(2,1)S(1)}, bf16[3,16,1024]{2,1,0:T(8,128)(2,1)S(1)}, u32[]{:S(2)}, u32[]{:S(2)}) collective-permute-start(bf16[3,16,1024]{2,1,0:T(8,128)(2,1)S(1)} %get-tuple-element.53), channel_id=1, source_target_pairs={{0,192},{4,196},{8,200},{12,204},{16,208},{20,212},{24,216},{28,22... | collective-permute-start | bytes 294920 | tf_op jit(solution)/shard_map/back/ppermute | solution.py:510
  95.7 0.6 collective-permute-start.14
  96.2 2.7 %collective-permute-done.11 = bf16[3,16,1024]{2,1,0:T(8,128)(2,1)S(1)} collective-permute-done((bf16[3,16,1024]{2,1,0:T(8,128)(2,1)S(1)}, bf16[3,16,1024]{2,1,0:T(8,128)(2,1)S(1)}, u32[]{:S(2)}, u32[]{:S(2)}) %collective-permute-start.11) | collective-permute-done | bytes 98336 | tf_op jit(solution)/shard_map/back/ppermute | solution.py:510
  98.9 2.3 %collective-permute-done.12 = bf16[3,16,1024]{2,1,0:T(8,128)(2,1)S(1)} collective-permute-done((bf16[3,16,1024]{2,1,0:T(8,128)(2,1)S(1)}, bf16[3,16,1024]{2,1,0:T(8,128)(2,1)S(1)}, u32[]{:S(2)}, u32[]{:S(2)}) %collective-permute-start.12) | collective-permute-done | bytes 98336 | tf_op jit(solution)/shard_map/back/ppermute | solution.py:510
  101.2 1.2 %collective-permute-done.14 = bf16[3,16,1024]{2,1,0:T(8,128)(2,1)S(1)} collective-permute-done((bf16[3,16,1024]{2,1,0:T(8,128)(2,1)S(1)}, bf16[3,16,1024]{2,1,0:T(8,128)(2,1)S(1)}, u32[]{:S(2)}, u32[]{:S(2)}) %collective-permute-start.14) | collective-permute-done | bytes 98336 | tf_op jit(solution)/shard_map/back/ppermute | solution.py:510
  102.4 3.6 %order_rows.1 = f32[512,1024]{1,0:T(8,128)} custom-call(bf16[640,1024]{1,0:T(8,128)(2,1)S(1)} %bitcast.14, bf16[48,1024]{1,0:T(8,128)(2,1)S(1)} %bitcast.15, bf16[48,1024]{1,0:T(8,128)(2,1)S(1)} %bitcast.16, bf16[48,1024]{1,0:T(8,128)(2,1)S(1)} %bitcast.17, bf16[48,1024]{1,0:T(8,128)(2,1)S(1)} %bitcast.18, bf16[48,1024]{1,0:T(8,128)(2,1)S(1)} %bitcast.19, ...), custom_call_target="tpu_custom_call" | custom-call | flops 1073741824 | bytes 4194304 | tf_op jit(solution)/shard_map/order/order_rows/pallas_call | solution.py:424
  (24 shorter events, 0.1 us)
Async XLA Ops:
  2.1 9.8 %copy-start.5 = (f32[32,1,4224]{2,1,0:T(1,128)S(1)}, f32[32,1,4224]{2,1,0:T(1,128)}, u32[]{:S(2)}) copy-start(f32[32,1,4224]{2,1,0:T(1,128)} %get-tuple-element.31) | copy-start | bytes 1622020
  2.1 30.6 %copy-start.3 = (f32[2,4]{1,0:T(2,128)S(1)}, f32[2,4]{1,0:T(2,128)}, u32[]{:S(2)}) copy-start(f32[2,4]{1,0:T(2,128)} %antenna_ref.1) | copy-start | bytes 100
  2.1 31.2 %copy-start = (bf16[16,256,512]{2,1,0:T(8,128)(2,1)S(1)}, bf16[16,256,512]{2,1,0:T(8,128)(2,1)}, u32[]{:S(2)}) copy-start(bf16[16,256,512]{2,1,0:T(8,128)(2,1)} %constant.2.clone.refs_4_.refs_3_.source) | copy-start | bytes 12582916
  2.1 31.2 %copy-start.2 = (f32[8,512]{1,0:T(8,128)S(1)}, f32[8,512]{1,0:T(8,128)}, u32[]{:S(2)}) copy-start(f32[8,512]{1,0:T(8,128)} %get-tuple-element.38.refs_5_.refs_8_) | copy-start | bytes 49156
  5.5 25.4 %collective-permute-start.1 = (bf16[64,4096]{1,0:T(8,128)(2,1)}, bf16[64,4096]{1,0:T(8,128)(2,1)S(1)}, u32[]{:S(2)}, u32[]{:S(2)}) collective-permute-start(bf16[64,4096]{1,0:T(8,128)(2,1)} %prepare_bank.1.refs_0_), channel_id=1, source_target_pairs={{0,8},{4,12},{8,16},{12,20},{16,24},{20,28},{24,32},{28,36},{32,40... | collective-permute-start | bytes 1572872 | tf_op jit(solution)/shard_map/ring/ppermute | solution.py:463
  8.0 22.9 %collective-permute-start = (bf16[64,4096]{1,0:T(8,128)(2,1)}, bf16[64,4096]{1,0:T(8,128)(2,1)S(1)}, u32[]{:S(2)}, u32[]{:S(2)}) collective-permute-start(bf16[64,4096]{1,0:T(8,128)(2,1)} %prepare_bank.1.refs_0_), channel_id=1, source_target_pairs={{0,56},{4,60},{8,0},{12,4},{16,8},{20,12},{24,16},{28,20},{32,24},... | collective-permute-start | bytes 1572872 | tf_op jit(solution)/shard_map/ring/ppermute | solution.py:464
  30.9 15.7 %collective-permute-start.2 = (bf16[64,4096]{1,0:T(8,128)(2,1)S(1)}, bf16[64,4096]{1,0:T(8,128)(2,1)S(1)}, u32[]{:S(2)}, u32[]{:S(2)}) collective-permute-start(bf16[64,4096]{1,0:T(8,128)(2,1)S(1)} %collective-permute-done.refs_2_), channel_id=1, source_target_pairs={{0,56},{4,60},{8,0},{12,4},{16,8},{20,12},{24,16},{28,20},{32,24},... | collective-permute-start | bytes 1572872 | tf_op jit(solution)/shard_map/ring/ppermute | solution.py:464
  32.6 14.0 %collective-permute-start.3 = (bf16[64,4096]{1,0:T(8,128)(2,1)S(1)}, bf16[64,4096]{1,0:T(8,128)(2,1)}, u32[]{:S(2)}, u32[]{:S(2)}) collective-permute-start(bf16[64,4096]{1,0:T(8,128)(2,1)S(1)} %collective-permute-done.1.refs_1_), channel_id=1, source_target_pairs={{0,8},{4,12},{8,16},{12,20},{16,24},{20,28},{24,32},{28,36},{32,40... | collective-permute-start | bytes 1572872 | tf_op jit(solution)/shard_map/ring/ppermute | solution.py:463
  33.3 1.0 copy-start.4
  46.6 17.3 %collective-permute-start.5 = (bf16[64,4096]{1,0:T(8,128)(2,1)}, bf16[64,4096]{1,0:T(8,128)(2,1)S(1)}, u32[]{:S(2)}, u32[]{:S(2)}) collective-permute-start(bf16[64,4096]{1,0:T(8,128)(2,1)} %collective-permute-done.3.refs_0_), channel_id=1, source_target_pairs={{0,8},{4,12},{8,16},{12,20},{16,24},{20,28},{24,32},{28,36},{32,40... | collective-permute-start | bytes 1572872 | tf_op jit(solution)/shard_map/ring/ppermute | solution.py:463
  46.7 17.2 %collective-permute-start.4 = (bf16[64,4096]{1,0:T(8,128)(2,1)S(1)}, bf16[64,4096]{1,0:T(8,128)(2,1)S(1)}, u32[]{:S(2)}, u32[]{:S(2)}) collective-permute-start(bf16[64,4096]{1,0:T(8,128)(2,1)S(1)} %collective-permute-done.2.refs_1_), channel_id=1, source_target_pairs={{0,56},{4,60},{8,0},{12,4},{16,8},{20,12},{24,16},{28,20},{32,24},... | collective-permute-start | bytes 1572872 | tf_op jit(solution)/shard_map/ring/ppermute | solution.py:464
  58.4 44.0 %all-to-all-start.1 = ((bf16[8,80,1024]{2,1,0:T(8,128)(2,1)}), bf16[8,80,1024]{2,1,0:T(8,128)(2,1)S(1)}, u32[]{:S(2)}, u32[]{:S(2)}) async-start(bf16[8,80,1024]{2,1,0:T(8,128)(2,1)} %bitcast.3), calls=%async_computation.1 | async-start | bytes 2621440 | tf_op jit(solution)/shard_map/back/all_to_all | solution.py:491
  64.0 7.8 %collective-permute-start.7 = (bf16[32,4096]{1,0:T(8,128)(2,1)S(1)}, bf16[32,4096]{1,0:T(8,128)(2,1)S(1)}, u32[]{:S(2)}, u32[]{:S(2)}) collective-permute-start(bf16[32,4096]{1,0:T(8,128)(2,1)S(1)} %slice.7), channel_id=1, source_target_pairs={{0,56},{4,60},{8,0},{12,4},{16,8},{20,12},{24,16},{28,20},{32,24},... | collective-permute-start | bytes 786440 | tf_op jit(solution)/shard_map/ring/ppermute | solution.py:467
  65.5 8.7 %collective-permute-start.6 = (bf16[32,4096]{1,0:T(8,128)(2,1)S(1)}, bf16[32,4096]{1,0:T(8,128)(2,1)S(1)}, u32[]{:S(2)}, u32[]{:S(2)}) collective-permute-start(bf16[32,4096]{1,0:T(8,128)(2,1)S(1)} %slice.6), channel_id=1, source_target_pairs={{0,8},{4,12},{8,16},{12,20},{16,24},{20,28},{24,32},{28,36},{32,40... | collective-permute-start | bytes 786440 | tf_op jit(solution)/shard_map/ring/ppermute | solution.py:467
  65.5 2.2 %copy-start.1 = (bf16[16,256,512]{2,1,0:T(8,128)(2,1)S(1)}, bf16[16,256,512]{2,1,0:T(8,128)(2,1)}, u32[]{:S(2)}) copy-start(bf16[16,256,512]{2,1,0:T(8,128)(2,1)} %constant.2.clone.refs_4_.refs_3_.source) | copy-start | bytes 12582916
  86.6 7.5 %collective-permute-start.8 = (bf16[3,16,1024]{2,1,0:T(8,128)(2,1)S(1)}, bf16[3,16,1024]{2,1,0:T(8,128)(2,1)S(1)}, u32[]{:S(2)}, u32[]{:S(2)}) collective-permute-start(bf16[3,16,1024]{2,1,0:T(8,128)(2,1)S(1)} %get-tuple-element.48), channel_id=1, source_target_pairs={{0,4},{4,0},{8,12},{12,8},{16,20},{20,16},{24,28},{28,24},{32,36},... | collective-permute-start | bytes 294920 | tf_op jit(solution)/shard_map/back/ppermute | solution.py:510
  88.0 7.7 %collective-permute-start.9 = (bf16[3,16,1024]{2,1,0:T(8,128)(2,1)S(1)}, bf16[3,16,1024]{2,1,0:T(8,128)(2,1)S(1)}, u32[]{:S(2)}, u32[]{:S(2)}) collective-permute-start(bf16[3,16,1024]{2,1,0:T(8,128)(2,1)S(1)} %get-tuple-element.49), channel_id=1, source_target_pairs={{0,64},{4,68},{8,72},{12,76},{16,80},{20,84},{24,88},{28,92},{32,9... | collective-permute-start | bytes 294920 | tf_op jit(solution)/shard_map/back/ppermute | solution.py:510
  89.4 6.8 %collective-permute-start.10 = (bf16[3,16,1024]{2,1,0:T(8,128)(2,1)S(1)}, bf16[3,16,1024]{2,1,0:T(8,128)(2,1)S(1)}, u32[]{:S(2)}, u32[]{:S(2)}) collective-permute-start(bf16[3,16,1024]{2,1,0:T(8,128)(2,1)S(1)} %get-tuple-element.50), channel_id=1, source_target_pairs={{0,68},{4,64},{8,76},{12,72},{16,84},{20,80},{24,92},{28,88},{32,1... | collective-permute-start | bytes 294920 | tf_op jit(solution)/shard_map/back/ppermute | solution.py:510
  90.8 8.1 %collective-permute-start.11 = (bf16[3,16,1024]{2,1,0:T(8,128)(2,1)S(1)}, bf16[3,16,1024]{2,1,0:T(8,128)(2,1)S(1)}, u32[]{:S(2)}, u32[]{:S(2)}) collective-permute-start(bf16[3,16,1024]{2,1,0:T(8,128)(2,1)S(1)} %get-tuple-element.51), channel_id=1, source_target_pairs={{0,128},{4,132},{8,136},{12,140},{16,144},{20,148},{24,152},{28,15... | collective-permute-start | bytes 294920 | tf_op jit(solution)/shard_map/back/ppermute | solution.py:510
  92.1 9.1 %collective-permute-start.12 = (bf16[3,16,1024]{2,1,0:T(8,128)(2,1)S(1)}, bf16[3,16,1024]{2,1,0:T(8,128)(2,1)S(1)}, u32[]{:S(2)}, u32[]{:S(2)}) collective-permute-start(bf16[3,16,1024]{2,1,0:T(8,128)(2,1)S(1)} %get-tuple-element.52), channel_id=1, source_target_pairs={{0,132},{4,128},{8,140},{12,136},{16,148},{20,144},{24,156},{28,15... | collective-permute-start | bytes 294920 | tf_op jit(solution)/shard_map/back/ppermute | solution.py:510
  94.2 7.1 %collective-permute-start.13 = (bf16[3,16,1024]{2,1,0:T(8,128)(2,1)S(1)}, bf16[3,16,1024]{2,1,0:T(8,128)(2,1)S(1)}, u32[]{:S(2)}, u32[]{:S(2)}) collective-permute-start(bf16[3,16,1024]{2,1,0:T(8,128)(2,1)S(1)} %get-tuple-element.53), channel_id=1, source_target_pairs={{0,192},{4,196},{8,200},{12,204},{16,208},{20,212},{24,216},{28,22... | collective-permute-start | bytes 294920 | tf_op jit(solution)/shard_map/back/ppermute | solution.py:510
  95.7 6.7 %collective-permute-start.14 = (bf16[3,16,1024]{2,1,0:T(8,128)(2,1)S(1)}, bf16[3,16,1024]{2,1,0:T(8,128)(2,1)S(1)}, u32[]{:S(2)}, u32[]{:S(2)}) collective-permute-start(bf16[3,16,1024]{2,1,0:T(8,128)(2,1)S(1)} %get-tuple-element.54), channel_id=1, source_target_pairs={{0,196},{4,192},{8,204},{12,200},{16,212},{20,208},{24,220},{28,21... | collective-permute-start | bytes 294920 | tf_op jit(solution)/shard_map/back/ppermute | solution.py:510

commit v2 on v1

--- a/solution.py
+++ b/solution.py
@@ -58,7 +58,9 @@
     return out
 
 
-def head_kernel(delays_ref, strain_ref, owner_ref, slot_ref, packet_ref, place_ref):
+def head_kernel(
+    dur_ref, delays_ref, bank_ref, strain_ref, owner_ref, slot_ref, own_ref, packet_ref, place_ref
+):
     det, my_z = lax.axis_index("det"), (lax.axis_index("seg") // NC) % NZ
     owner = owner_ref[...]
     n = owner.shape[1]
@@ -115,11 +117,6 @@
             packet_ref[m, :, 0:WIDE] = shifted
         packet_ref[m, :, WIDE:] = table[m // ND : m // ND + 1, :]
 
-
-def bank_kernel(dur_ref, bank_ref, out_ref):
-    row16 = lax.broadcasted_iota(jnp.int32, (16, 128), 0)
-    lane16 = lax.broadcasted_iota(jnp.int32, (16, 128), 1)
-
     def rows(i, _):
         r = pl.ds(pl.multiple_of(i * 16, 16), 16)
         dur = jnp.zeros((16, 128), jnp.int32)
@@ -133,41 +130,29 @@
             x = to_classes(x, lane16)
             for f2 in range(CLASSES):
                 at = f2 * 256 + c * 128
-                out_ref[r, at : at + 128] = x[f2].astype(jnp.bfloat16)
+                own_ref[r, at : at + 128] = x[f2].astype(jnp.bfloat16)
         return 0
 
     lax.fori_loop(0, SLOTS // 16, rows, 0)
 
 
-def head(delays, strain, owner, slot):
+def head(dur, delays, bank, strain, owner, slot):
     n = owner.shape[1]
     vmem = pl.BlockSpec(memory_space=pltpu.VMEM)
     smem = pl.BlockSpec(memory_space=pltpu.SMEM)
     return pl.pallas_call(
         head_kernel,
         out_shape=[
+            jax.ShapeDtypeStruct((SLOTS, WIDE), jnp.bfloat16),
             jax.ShapeDtypeStruct((PEERS * ND, 1, WIDE + 128), jnp.float32),
             jax.ShapeDtypeStruct((8, n), jnp.float32),
         ],
-        in_specs=[smem] + [vmem] * 3,
-        out_specs=[vmem] * 2,
-        compiler_params=pltpu.CompilerParams(vmem_limit_bytes=58 << 20),
-        cost_estimate=pl.CostEstimate(flops=4 << 20, bytes_accessed=2 << 20, transcendentals=0),
-        name="head",
-    )(delays, strain, owner, slot)
-
-
-def prepare_bank(dur, bank):
-    vmem = pl.BlockSpec(memory_space=pltpu.VMEM)
-    return pl.pallas_call(
-        bank_kernel,
-        out_shape=jax.ShapeDtypeStruct((SLOTS, WIDE), jnp.bfloat16),
-        in_specs=[pl.BlockSpec(memory_space=pltpu.SMEM), vmem],
-        out_specs=vmem,
+        in_specs=[smem] * 2 + [vmem] * 4,
+        out_specs=[vmem] * 3,
         compiler_params=pltpu.CompilerParams(vmem_limit_bytes=58 << 20),
         cost_estimate=pl.CostEstimate(flops=8 << 30, bytes_accessed=2 << 20, transcendentals=0),
-        name="prepare_bank",
-    )(dur, bank)
+        name="head",
+    )(dur, delays, bank, strain, owner, slot)
 
 
 def combine_kernel(antenna_ref, packet_ref, out_ref):
@@ -191,7 +176,7 @@
         in_specs=[smem, vmem],
         out_specs=vmem,
         compiler_params=pltpu.CompilerParams(vmem_limit_bytes=16 << 20),
-        cost_estimate=pl.CostEstimate(flops=1 << 20, bytes_accessed=1 << 20, transcendentals=0),
+        cost_estimate=pl.CostEstimate(flops=4 << 30, bytes_accessed=1 << 20, transcendentals=0),
         name="combine",
     )(antenna, packet)
 
@@ -336,7 +321,7 @@
                     out_ref[s, i, :, q * T1 + h * 128 : q * T1 + (h + 1) * 128] = v
             return 0
 
-        lax.fori_loop(0, PEERS, tile, 0, unroll=2)
+        lax.fori_loop(0, PEERS, tile, 0, unroll=4)
         return 0
 
     lax.fori_loop(0, count, block, 0)
@@ -419,7 +404,7 @@
 
 def order_rows(near, pieces, place):
     n = place.shape[1]
-    step = 128
+    step = 256
     whole = [pl.BlockSpec(r.shape, lambda i: (0, 0)) for r in [near, *pieces]]
     return pl.pallas_call(
         order_kernel,
@@ -447,13 +432,14 @@
     half = SLOTS // 2
 
     with jax.named_scope("head"):
-        packet, place = head(
-            delays, strain.reshape(WIDE // 128, 128), owner_seg.reshape(1, -1), slot_index
+        own, packet, place = head(
+            duration_bin,
+            delays,
+            template_bank[0],
+            strain.reshape(WIDE // 128, 128),
+            owner_seg.reshape(1, -1),
+            slot_index,
         )
-
-    packet, template_bank = lax.optimization_barrier((packet, template_bank))
-    with jax.named_scope("bank"):
-        own = prepare_bank(duration_bin, template_bank[0])
 
     held = {0: own}
 

time: 106 us -> 103 us (0.972)
  Pallas kernels: 43.6 us -> 41.1 us
    pallas_call x2 -> x1, Pallas kernels: 5.47 us -> 3.75 us  [head(): pl.pallas_call(head_kernel, out_shape=[jax.ShapeDtypeStruct((SLOTS, WIDE)...]
    ppermute x1, waiting for transfers between devices: 2.31 us -> 1.18 us  [ring(): lax.ppermute(held[-3][:half], 'seg', up)]
    ppermute x1, starting transfers between devices: 0.04 us -> 1.17 us  [ring(): lax.ppermute(held[-3][:half], 'seg', up)]
    unnamed x12 -> x10, local copies, waits for them, and re-layouts: 3.24 us -> 2.2 us
  transfers between devices with their start and end apart: 16 -> 16, of which waited for: 5 -> 6; matrix products, arithmetic and copies ran while one was open for 0% -> 0% of each run, Pallas kernels for 33% -> 33%
where the time goes in v2:
time: 103 us
  Pallas kernels  41.1 us (40%)
  starting transfers between devices  28.4 us (28%)
  blocking collectives  19.2 us (19%)
  waiting for transfers between devices  11.8 us (11%)
  local copies, waits for them, and re-layouts  2.24 us (2%)
    pallas_call x3, Pallas kernels, filter_banks(): pl.pallas_call(functools.partial(filter_kernel, count, first, slot, sprea...  33.3 us
    all_to_all x1, blocking collectives, per_device(): lax.all_to_all(packet, ('seg', 'det'), split_axis=0, concat_axis=0, tiled...  19.2 us
    ppermute x7, starting transfers between devices, per_device(): pieces[k] = lax.ppermute(pieces[k], 'seg', to)  9.55 us
    ppermute x3, starting transfers between devices, ring(): held[k] = lax.ppermute(held[k - 1], 'seg', down)  8.43 us
    all_to_all x1, starting transfers between devices, per_device(): lax.all_to_all(rows.reshape(PEERS, slot * CAP, STEP), 'seg', split_axis=0...  6.25 us
    ppermute x7, waiting for transfers between devices, per_device(): pieces[k] = lax.ppermute(pieces[k], 'seg', to)  6.16 us
    ppermute x1, waiting for transfers between devices, ring(): lax.ppermute(held[3][half:], 'seg', down)  3.82 us
    pallas_call x1, Pallas kernels, head(): pl.pallas_call(head_kernel, out_shape=[jax.ShapeDtypeStruct((SLOTS, WIDE)...  3.75 us
  transfers between devices with their start and end apart: 16, of which 6 were waited for; matrix products, arithmetic and copies ran while one was open for 0% of the time, Pallas kernels for 33%

profile of v2, /device:TPU:1, one launch (start us, length us, event | category | flops | bytes accessed | tf_op | source)
XLA Modules:
  0.0 102.9 jit_solution(4176125603548520983)
XLA Ops:
  0.0 3.7 %head.1 = (bf16[64,4096]{1,0:T(8,128)(2,1)}, f32[32,1,4224]{2,1,0:T(1,128)}, f32[8,512]{1,0:T(8,128)}) custom-call(s32[1,64]{1,0:T(1,128)} %dur_ref.1, s32[4]{0:T(128)} %delays_ref.1, bf16[64,4096]{1,0:T(8,128)(2,1)} %bitcast.23, f32[32,128]{1,0:T(8,128)} %bitcast.24, s32[1,512]{1,0:T(1,128)} %bitcast.25, s32[1,512]{1,0:T(1,128)} %slot_ref.1), custom_call_target="tpu_custom_call" | custom-call | flops 8589934592 | bytes 2097152 | tf_op jit(solution)/shard_map/head/head/pallas_call | solution.py:143
  3.7 2.5 %collective-permute-start.1 = (bf16[64,4096]{1,0:T(8,128)(2,1)}, bf16[64,4096]{1,0:T(8,128)(2,1)S(1)}, u32[]{:S(2)}, u32[]{:S(2)}) collective-permute-start(bf16[64,4096]{1,0:T(8,128)(2,1)} %get-tuple-element.30.refs_0_), channel_id=1, source_target_pairs={{0,8},{4,12},{8,16},{12,20},{16,24},{20,28},{24,32},{28,36},{32,40... | collective-permute-start | bytes 1572872 | tf_op jit(solution)/shard_map/ring/ppermute | solution.py:449
  6.2 3.9 %collective-permute-start = (bf16[64,4096]{1,0:T(8,128)(2,1)}, bf16[64,4096]{1,0:T(8,128)(2,1)S(1)}, u32[]{:S(2)}, u32[]{:S(2)}) collective-permute-start(bf16[64,4096]{1,0:T(8,128)(2,1)} %get-tuple-element.30.refs_0_), channel_id=1, source_target_pairs={{0,56},{4,60},{8,0},{12,4},{16,8},{20,12},{24,16},{28,20},{32,24},... | collective-permute-start | bytes 1572872 | tf_op jit(solution)/shard_map/ring/ppermute | solution.py:450
  10.2 19.2 %all_to_all.10.packet_ref = f32[32,1,4224]{2,1,0:T(1,128)S(1)} all-to-all(f32[32,1,4224]{2,1,0:T(1,128)} %get-tuple-element.29), channel_id=1, replica_groups={{0,1,2,3,4,5,6,7,64,65,66,67,68,69,70,71,128,129,130,131,132,133,134,13..., dimensions={0} | all-to-all | bytes 1081344 | tf_op jit(solution)/shard_map/exchange/all_to_all | solution.py:458
  29.4 1.8 %collective-permute-start.2 = (bf16[64,4096]{1,0:T(8,128)(2,1)S(1)}, bf16[64,4096]{1,0:T(8,128)(2,1)S(1)}, u32[]{:S(2)}, u32[]{:S(2)}) collective-permute-start(bf16[64,4096]{1,0:T(8,128)(2,1)S(1)} %collective-permute-done.refs_2_), channel_id=1, source_target_pairs={{0,56},{4,60},{8,0},{12,4},{16,8},{20,12},{24,16},{28,20},{32,24},... | collective-permute-start | bytes 1572872 | tf_op jit(solution)/shard_map/ring/ppermute | solution.py:450
  31.2 0.6 combine.1.refs_3_.refs_2_
  31.9 12.1 %filter3_0.1 = (bf16[8,5,16,1024]{3,2,1,0:T(8,128)(2,1)}, f32[8,128]{1,0:T(8,128)}) custom-call(bf16[64,4096]{1,0:T(8,128)(2,1)S(1)} %copy-done.3, bf16[64,4096]{1,0:T(8,128)(2,1)S(1)} %collective-permute-done.1.refs_1_, bf16[64,4096]{1,0:T(8,128)(2,1)S(1)} %collective-permute-done.refs_2_, f32[8,1,8320]{2,1,0:T(1,128)S(1)} %combine.1.refs_3_.refs_2_, ...), custom_call_target="tpu_custom_call" | custom-call | flops 9663676416 | bytes 1048576 | tf_op jit(solution)/shard_map/filter/filter3_0/pallas_call | solution.py:351
  44.0 0.6 collective-permute-done.3.refs_0_
  44.6 0.0 collective-permute-start.5
  44.7 2.7 %collective-permute-start.4 = (bf16[64,4096]{1,0:T(8,128)(2,1)S(1)}, bf16[64,4096]{1,0:T(8,128)(2,1)S(1)}, u32[]{:S(2)}, u32[]{:S(2)}) collective-permute-start(bf16[64,4096]{1,0:T(8,128)(2,1)S(1)} %collective-permute-done.2.refs_1_), channel_id=1, source_target_pairs={{0,56},{4,60},{8,0},{12,4},{16,8},{20,12},{24,16},{28,20},{32,24},... | collective-permute-start | bytes 1572872 | tf_op jit(solution)/shard_map/ring/ppermute | solution.py:450
  47.3 8.8 %filter2_48.1 = (bf16[8,5,16,1024]{3,2,1,0:T(8,128)(2,1)}, f32[8,128]{1,0:T(8,128)S(1)}) custom-call(bf16[64,4096]{1,0:T(8,128)(2,1)} %collective-permute-done.3.refs_0_, bf16[64,4096]{1,0:T(8,128)(2,1)S(1)} %collective-permute-done.2.refs_1_, f32[8,1,8320]{2,1,0:T(1,128)S(1)} %combine.1.refs_3_.refs_2_, ...), custom_call_target="tpu_custom_call", output_to_operand_aliasing={{0}: (4, {})} | custom-call | flops 6442450944 | bytes 1048576 | tf_op jit(solution)/shard_map/filter/filter2_48/pallas_call | solution.py:351
  56.2 6.3 %all-to-all-start.1 = ((bf16[8,80,1024]{2,1,0:T(8,128)(2,1)}), bf16[8,80,1024]{2,1,0:T(8,128)(2,1)S(1)}, u32[]{:S(2)}, u32[]{:S(2)}) async-start(bf16[8,80,1024]{2,1,0:T(8,128)(2,1)} %bitcast.3), calls=%async_computation.1 | async-start | bytes 2621440 | tf_op jit(solution)/shard_map/back/all_to_all | solution.py:477
  62.5 0.6 collective-permute-start.7
  63.0 1.2 %collective-permute-start.6 = (bf16[32,4096]{1,0:T(8,128)(2,1)S(1)}, bf16[32,4096]{1,0:T(8,128)(2,1)S(1)}, u32[]{:S(2)}, u32[]{:S(2)}) collective-permute-start(bf16[32,4096]{1,0:T(8,128)(2,1)S(1)} %slice.6), channel_id=1, source_target_pairs={{0,8},{4,12},{8,16},{12,20},{16,24},{20,28},{24,32},{28,36},{32,40... | collective-permute-start | bytes 786440 | tf_op jit(solution)/shard_map/ring/ppermute | solution.py:453
  64.2 2.2 %copy-done.1 = bf16[16,256,512]{2,1,0:T(8,128)(2,1)S(1)} copy-done((bf16[16,256,512]{2,1,0:T(8,128)(2,1)S(1)}, bf16[16,256,512]{2,1,0:T(8,128)(2,1)}, u32[]{:S(2)}) %copy-start.1) | copy-done | bytes 4194328
  66.4 0.3 stage_basis.1.refs_4_
  66.7 3.8 %collective-permute-done.7 = bf16[32,4096]{1,0:T(8,128)(2,1)S(1)} collective-permute-done((bf16[32,4096]{1,0:T(8,128)(2,1)S(1)}, bf16[32,4096]{1,0:T(8,128)(2,1)S(1)}, u32[]{:S(2)}, u32[]{:S(2)}) %collective-permute-start.7) | collective-permute-done | bytes 262176 | tf_op jit(solution)/shard_map/ring/ppermute | solution.py:453
  70.5 1.2 %collective-permute-done.6 = bf16[32,4096]{1,0:T(8,128)(2,1)S(1)} collective-permute-done((bf16[32,4096]{1,0:T(8,128)(2,1)S(1)}, bf16[32,4096]{1,0:T(8,128)(2,1)S(1)}, u32[]{:S(2)}, u32[]{:S(2)}) %collective-permute-start.6) | collective-permute-done | bytes 262176 | tf_op jit(solution)/shard_map/ring/ppermute | solution.py:453
  71.7 12.3 %filter3_80.1 = (bf16[3,16,1024]{2,1,0:T(8,128)(2,1)S(1)}, bf16[3,16,1024]{2,1,0:T(8,128)(2,1)S(1)}, bf16[3,16,1024]{2,1,0:T(8,128)(2,1)S(1)}, bf16[3,16,1024]{2...) custom-call(bf16[64,4096]{1,0:T(8,128)(2,1)S(1)} %collective-permute, ...), custom_call_target="tpu_custom_call" | custom-call | bytes 1048576 | tf_op jit(solution)/shard_map/filter/filter3_80/pallas_call | solution.py:351
  84.1 1.3 %collective-permute-start.8 = (bf16[3,16,1024]{2,1,0:T(8,128)(2,1)S(1)}, bf16[3,16,1024]{2,1,0:T(8,128)(2,1)S(1)}, u32[]{:S(2)}, u32[]{:S(2)}) collective-permute-start(bf16[3,16,1024]{2,1,0:T(8,128)(2,1)S(1)} %get-tuple-element.46), channel_id=1, source_target_pairs={{0,4},{4,0},{8,12},{12,8},{16,20},{20,16},{24,28},{28,24},{32,36},... | collective-permute-start | bytes 294920 | tf_op jit(solution)/shard_map/back/ppermute | solution.py:496
  85.4 1.4 %collective-permute-start.9 = (bf16[3,16,1024]{2,1,0:T(8,128)(2,1)S(1)}, bf16[3,16,1024]{2,1,0:T(8,128)(2,1)S(1)}, u32[]{:S(2)}, u32[]{:S(2)}) collective-permute-start(bf16[3,16,1024]{2,1,0:T(8,128)(2,1)S(1)} %get-tuple-element.47), channel_id=1, source_target_pairs={{0,64},{4,68},{8,72},{12,76},{16,80},{20,84},{24,88},{28,92},{32,9... | collective-permute-start | bytes 294920 | tf_op jit(solution)/shard_map/back/ppermute | solution.py:496
  86.8 1.5 %collective-permute-start.10 = (bf16[3,16,1024]{2,1,0:T(8,128)(2,1)S(1)}, bf16[3,16,1024]{2,1,0:T(8,128)(2,1)S(1)}, u32[]{:S(2)}, u32[]{:S(2)}) collective-permute-start(bf16[3,16,1024]{2,1,0:T(8,128)(2,1)S(1)} %get-tuple-element.48), channel_id=1, source_target_pairs={{0,68},{4,64},{8,76},{12,72},{16,84},{20,80},{24,92},{28,88},{32,1... | collective-permute-start | bytes 294920 | tf_op jit(solution)/shard_map/back/ppermute | solution.py:496
  88.3 1.3 %collective-permute-start.11 = (bf16[3,16,1024]{2,1,0:T(8,128)(2,1)S(1)}, bf16[3,16,1024]{2,1,0:T(8,128)(2,1)S(1)}, u32[]{:S(2)}, u32[]{:S(2)}) collective-permute-start(bf16[3,16,1024]{2,1,0:T(8,128)(2,1)S(1)} %get-tuple-element.49), channel_id=1, source_target_pairs={{0,128},{4,132},{8,136},{12,140},{16,144},{20,148},{24,152},{28,15... | collective-permute-start | bytes 294920 | tf_op jit(solution)/shard_map/back/ppermute | solution.py:496
  89.5 2.0 %collective-permute-start.12 = (bf16[3,16,1024]{2,1,0:T(8,128)(2,1)S(1)}, bf16[3,16,1024]{2,1,0:T(8,128)(2,1)S(1)}, u32[]{:S(2)}, u32[]{:S(2)}) collective-permute-start(bf16[3,16,1024]{2,1,0:T(8,128)(2,1)S(1)} %get-tuple-element.50), channel_id=1, source_target_pairs={{0,132},{4,128},{8,140},{12,136},{16,148},{20,144},{24,156},{28,15... | collective-permute-start | bytes 294920 | tf_op jit(solution)/shard_map/back/ppermute | solution.py:496
  91.6 1.5 %collective-permute-start.13 = (bf16[3,16,1024]{2,1,0:T(8,128)(2,1)S(1)}, bf16[3,16,1024]{2,1,0:T(8,128)(2,1)S(1)}, u32[]{:S(2)}, u32[]{:S(2)}) collective-permute-start(bf16[3,16,1024]{2,1,0:T(8,128)(2,1)S(1)} %get-tuple-element.51), channel_id=1, source_target_pairs={{0,192},{4,196},{8,200},{12,204},{16,208},{20,212},{24,216},{28,22... | collective-permute-start | bytes 294920 | tf_op jit(solution)/shard_map/back/ppermute | solution.py:496
  93.0 0.6 collective-permute-start.14
  93.6 0.0 collective-permute-done.10
  93.6 2.7 %collective-permute-done.11 = bf16[3,16,1024]{2,1,0:T(8,128)(2,1)S(1)} collective-permute-done((bf16[3,16,1024]{2,1,0:T(8,128)(2,1)S(1)}, bf16[3,16,1024]{2,1,0:T(8,128)(2,1)S(1)}, u32[]{:S(2)}, u32[]{:S(2)}) %collective-permute-start.11) | collective-permute-done | bytes 98336 | tf_op jit(solution)/shard_map/back/ppermute | solution.py:496
  96.3 2.3 %collective-permute-done.12 = bf16[3,16,1024]{2,1,0:T(8,128)(2,1)S(1)} collective-permute-done((bf16[3,16,1024]{2,1,0:T(8,128)(2,1)S(1)}, bf16[3,16,1024]{2,1,0:T(8,128)(2,1)S(1)}, u32[]{:S(2)}, u32[]{:S(2)}) %collective-permute-start.12) | collective-permute-done | bytes 98336 | tf_op jit(solution)/shard_map/back/ppermute | solution.py:496
  98.6 0.0 collective-permute-done.13
  98.6 1.2 %collective-permute-done.14 = bf16[3,16,1024]{2,1,0:T(8,128)(2,1)S(1)} collective-permute-done((bf16[3,16,1024]{2,1,0:T(8,128)(2,1)S(1)}, bf16[3,16,1024]{2,1,0:T(8,128)(2,1)S(1)}, u32[]{:S(2)}, u32[]{:S(2)}) %collective-permute-start.14) | collective-permute-done | bytes 98336 | tf_op jit(solution)/shard_map/back/ppermute | solution.py:496
  99.8 3.2 %order_rows.1 = f32[512,1024]{1,0:T(8,128)} custom-call(bf16[640,1024]{1,0:T(8,128)(2,1)S(1)} %bitcast.14, bf16[48,1024]{1,0:T(8,128)(2,1)S(1)} %bitcast.15, bf16[48,1024]{1,0:T(8,128)(2,1)S(1)} %bitcast.16, bf16[48,1024]{1,0:T(8,128)(2,1)S(1)} %bitcast.17, bf16[48,1024]{1,0:T(8,128)(2,1)S(1)} %bitcast.18, bf16[48,1024]{1,0:T(8,128)(2,1)S(1)} %bitcast.19, ...), custom_call_target="tpu_custom_call" | custom-call | flops 1073741824 | bytes 4194304 | tf_op jit(solution)/shard_map/order/order_rows/pallas_call | solution.py:409
  (21 shorter events, 0.1 us)
Async XLA Ops:
  0.0 31.2 %copy-start.4 = (f32[2,4]{1,0:T(2,128)S(1)}, f32[2,4]{1,0:T(2,128)}, u32[]{:S(2)}) copy-start(f32[2,4]{1,0:T(2,128)} %antenna_ref.1) | copy-start | bytes 100
  3.7 25.6 %collective-permute-start.1 = (bf16[64,4096]{1,0:T(8,128)(2,1)}, bf16[64,4096]{1,0:T(8,128)(2,1)S(1)}, u32[]{:S(2)}, u32[]{:S(2)}) collective-permute-start(bf16[64,4096]{1,0:T(8,128)(2,1)} %get-tuple-element.30.refs_0_), channel_id=1, source_target_pairs={{0,8},{4,12},{8,16},{12,20},{16,24},{20,28},{24,32},{28,36},{32,40... | collective-permute-start | bytes 1572872 | tf_op jit(solution)/shard_map/ring/ppermute | solution.py:449
  6.2 23.2 %collective-permute-start = (bf16[64,4096]{1,0:T(8,128)(2,1)}, bf16[64,4096]{1,0:T(8,128)(2,1)S(1)}, u32[]{:S(2)}, u32[]{:S(2)}) collective-permute-start(bf16[64,4096]{1,0:T(8,128)(2,1)} %get-tuple-element.30.refs_0_), channel_id=1, source_target_pairs={{0,56},{4,60},{8,0},{12,4},{16,8},{20,12},{24,16},{28,20},{32,24},... | collective-permute-start | bytes 1572872 | tf_op jit(solution)/shard_map/ring/ppermute | solution.py:450
  29.4 2.5 %copy-start = (bf16[16,256,512]{2,1,0:T(8,128)(2,1)S(1)}, bf16[16,256,512]{2,1,0:T(8,128)(2,1)}, u32[]{:S(2)}) copy-start(bf16[16,256,512]{2,1,0:T(8,128)(2,1)} %constant.2.clone.refs_4_.refs_3_.source) | copy-start | bytes 12582916
  29.4 2.5 %copy-start.2 = (f32[8,512]{1,0:T(8,128)S(1)}, f32[8,512]{1,0:T(8,128)}, u32[]{:S(2)}) copy-start(f32[8,512]{1,0:T(8,128)} %get-tuple-element.36.refs_5_.refs_8_) | copy-start | bytes 49156
  29.4 2.5 %copy-start.3 = (bf16[64,4096]{1,0:T(8,128)(2,1)S(1)}, bf16[64,4096]{1,0:T(8,128)(2,1)}, u32[]{:S(2)}) copy-start(bf16[64,4096]{1,0:T(8,128)(2,1)} %get-tuple-element.30.refs_0_) | copy-start | bytes 1572868
  29.4 14.6 %collective-permute-start.2 = (bf16[64,4096]{1,0:T(8,128)(2,1)S(1)}, bf16[64,4096]{1,0:T(8,128)(2,1)S(1)}, u32[]{:S(2)}, u32[]{:S(2)}) collective-permute-start(bf16[64,4096]{1,0:T(8,128)(2,1)S(1)} %collective-permute-done.refs_2_), channel_id=1, source_target_pairs={{0,56},{4,60},{8,0},{12,4},{16,8},{20,12},{24,16},{28,20},{32,24},... | collective-permute-start | bytes 1572872 | tf_op jit(solution)/shard_map/ring/ppermute | solution.py:450
  31.2 13.4 %collective-permute-start.3 = (bf16[64,4096]{1,0:T(8,128)(2,1)S(1)}, bf16[64,4096]{1,0:T(8,128)(2,1)}, u32[]{:S(2)}, u32[]{:S(2)}) collective-permute-start(bf16[64,4096]{1,0:T(8,128)(2,1)S(1)} %collective-permute-done.1.refs_1_), channel_id=1, source_target_pairs={{0,8},{4,12},{8,16},{12,20},{16,24},{20,28},{24,32},{28,36},{32,40... | collective-permute-start | bytes 1572872 | tf_op jit(solution)/shard_map/ring/ppermute | solution.py:449
  44.6 17.8 %collective-permute-start.5 = (bf16[64,4096]{1,0:T(8,128)(2,1)}, bf16[64,4096]{1,0:T(8,128)(2,1)S(1)}, u32[]{:S(2)}, u32[]{:S(2)}) collective-permute-start(bf16[64,4096]{1,0:T(8,128)(2,1)} %collective-permute-done.3.refs_0_), channel_id=1, source_target_pairs={{0,8},{4,12},{8,16},{12,20},{16,24},{20,28},{24,32},{28,36},{32,40... | collective-permute-start | bytes 1572872 | tf_op jit(solution)/shard_map/ring/ppermute | solution.py:449
  44.7 17.8 %collective-permute-start.4 = (bf16[64,4096]{1,0:T(8,128)(2,1)S(1)}, bf16[64,4096]{1,0:T(8,128)(2,1)S(1)}, u32[]{:S(2)}, u32[]{:S(2)}) collective-permute-start(bf16[64,4096]{1,0:T(8,128)(2,1)S(1)} %collective-permute-done.2.refs_1_), channel_id=1, source_target_pairs={{0,56},{4,60},{8,0},{12,4},{16,8},{20,12},{24,16},{28,20},{32,24},... | collective-permute-start | bytes 1572872 | tf_op jit(solution)/shard_map/ring/ppermute | solution.py:450
  56.2 43.6 %all-to-all-start.1 = ((bf16[8,80,1024]{2,1,0:T(8,128)(2,1)}), bf16[8,80,1024]{2,1,0:T(8,128)(2,1)S(1)}, u32[]{:S(2)}, u32[]{:S(2)}) async-start(bf16[8,80,1024]{2,1,0:T(8,128)(2,1)} %bitcast.3), calls=%async_computation.1 | async-start | bytes 2621440 | tf_op jit(solution)/shard_map/back/all_to_all | solution.py:477
  62.5 8.0 %collective-permute-start.7 = (bf16[32,4096]{1,0:T(8,128)(2,1)S(1)}, bf16[32,4096]{1,0:T(8,128)(2,1)S(1)}, u32[]{:S(2)}, u32[]{:S(2)}) collective-permute-start(bf16[32,4096]{1,0:T(8,128)(2,1)S(1)} %slice.7), channel_id=1, source_target_pairs={{0,56},{4,60},{8,0},{12,4},{16,8},{20,12},{24,16},{28,20},{32,24},... | collective-permute-start | bytes 786440 | tf_op jit(solution)/shard_map/ring/ppermute | solution.py:453
  63.0 8.7 %collective-permute-start.6 = (bf16[32,4096]{1,0:T(8,128)(2,1)S(1)}, bf16[32,4096]{1,0:T(8,128)(2,1)S(1)}, u32[]{:S(2)}, u32[]{:S(2)}) collective-permute-start(bf16[32,4096]{1,0:T(8,128)(2,1)S(1)} %slice.6), channel_id=1, source_target_pairs={{0,8},{4,12},{8,16},{12,20},{16,24},{20,28},{24,32},{28,36},{32,40... | collective-permute-start | bytes 786440 | tf_op jit(solution)/shard_map/ring/ppermute | solution.py:453
  64.2 2.2 %copy-start.1 = (bf16[16,256,512]{2,1,0:T(8,128)(2,1)S(1)}, bf16[16,256,512]{2,1,0:T(8,128)(2,1)}, u32[]{:S(2)}) copy-start(bf16[16,256,512]{2,1,0:T(8,128)(2,1)} %constant.2.clone.refs_4_.refs_3_.source) | copy-start | bytes 12582916
  84.1 7.5 %collective-permute-start.8 = (bf16[3,16,1024]{2,1,0:T(8,128)(2,1)S(1)}, bf16[3,16,1024]{2,1,0:T(8,128)(2,1)S(1)}, u32[]{:S(2)}, u32[]{:S(2)}) collective-permute-start(bf16[3,16,1024]{2,1,0:T(8,128)(2,1)S(1)} %get-tuple-element.46), channel_id=1, source_target_pairs={{0,4},{4,0},{8,12},{12,8},{16,20},{20,16},{24,28},{28,24},{32,36},... | collective-permute-start | bytes 294920 | tf_op jit(solution)/shard_map/back/ppermute | solution.py:496
  85.4 7.6 %collective-permute-start.9 = (bf16[3,16,1024]{2,1,0:T(8,128)(2,1)S(1)}, bf16[3,16,1024]{2,1,0:T(8,128)(2,1)S(1)}, u32[]{:S(2)}, u32[]{:S(2)}) collective-permute-start(bf16[3,16,1024]{2,1,0:T(8,128)(2,1)S(1)} %get-tuple-element.47), channel_id=1, source_target_pairs={{0,64},{4,68},{8,72},{12,76},{16,80},{20,84},{24,88},{28,92},{32,9... | collective-permute-start | bytes 294920 | tf_op jit(solution)/shard_map/back/ppermute | solution.py:496
  86.8 6.8 %collective-permute-start.10 = (bf16[3,16,1024]{2,1,0:T(8,128)(2,1)S(1)}, bf16[3,16,1024]{2,1,0:T(8,128)(2,1)S(1)}, u32[]{:S(2)}, u32[]{:S(2)}) collective-permute-start(bf16[3,16,1024]{2,1,0:T(8,128)(2,1)S(1)} %get-tuple-element.48), channel_id=1, source_target_pairs={{0,68},{4,64},{8,76},{12,72},{16,84},{20,80},{24,92},{28,88},{32,1... | collective-permute-start | bytes 294920 | tf_op jit(solution)/shard_map/back/ppermute | solution.py:496
  88.3 8.1 %collective-permute-start.11 = (bf16[3,16,1024]{2,1,0:T(8,128)(2,1)S(1)}, bf16[3,16,1024]{2,1,0:T(8,128)(2,1)S(1)}, u32[]{:S(2)}, u32[]{:S(2)}) collective-permute-start(bf16[3,16,1024]{2,1,0:T(8,128)(2,1)S(1)} %get-tuple-element.49), channel_id=1, source_target_pairs={{0,128},{4,132},{8,136},{12,140},{16,144},{20,148},{24,152},{28,15... | collective-permute-start | bytes 294920 | tf_op jit(solution)/shard_map/back/ppermute | solution.py:496
  89.5 9.1 %collective-permute-start.12 = (bf16[3,16,1024]{2,1,0:T(8,128)(2,1)S(1)}, bf16[3,16,1024]{2,1,0:T(8,128)(2,1)S(1)}, u32[]{:S(2)}, u32[]{:S(2)}) collective-permute-start(bf16[3,16,1024]{2,1,0:T(8,128)(2,1)S(1)} %get-tuple-element.50), channel_id=1, source_target_pairs={{0,132},{4,128},{8,140},{12,136},{16,148},{20,144},{24,156},{28,15... | collective-permute-start | bytes 294920 | tf_op jit(solution)/shard_map/back/ppermute | solution.py:496
  91.6 7.0 %collective-permute-start.13 = (bf16[3,16,1024]{2,1,0:T(8,128)(2,1)S(1)}, bf16[3,16,1024]{2,1,0:T(8,128)(2,1)S(1)}, u32[]{:S(2)}, u32[]{:S(2)}) collective-permute-start(bf16[3,16,1024]{2,1,0:T(8,128)(2,1)S(1)} %get-tuple-element.51), channel_id=1, source_target_pairs={{0,192},{4,196},{8,200},{12,204},{16,208},{20,212},{24,216},{28,22... | collective-permute-start | bytes 294920 | tf_op jit(solution)/shard_map/back/ppermute | solution.py:496
  93.0 6.7 %collective-permute-start.14 = (bf16[3,16,1024]{2,1,0:T(8,128)(2,1)S(1)}, bf16[3,16,1024]{2,1,0:T(8,128)(2,1)S(1)}, u32[]{:S(2)}, u32[]{:S(2)}) collective-permute-start(bf16[3,16,1024]{2,1,0:T(8,128)(2,1)S(1)} %get-tuple-element.52), channel_id=1, source_target_pairs={{0,196},{4,192},{8,204},{12,200},{16,212},{20,208},{24,220},{28,21... | collective-permute-start | bytes 294920 | tf_op jit(solution)/shard_map/back/ppermute | solution.py:496

commit v3 on v2

--- a/solution.py
+++ b/solution.py
@@ -21,7 +21,7 @@
 T1 = 256
 QS = 4
 BIG = 3.0e38
-CALLS = {(0, -1, 1, -2, 2): ((0, -1, 1), (-2, 2)), (-3, 3, 4): ((-3, 3, 4),)}
+CALLS = {(0, -1, 1, -2, 2): ((0, -1, 1), (-2, 2)), (-3, 3, 4): ((-3, 3), (4,))}
 PARTS = tuple(CALLS)
 
 LANE = np.arange(128)
@@ -244,7 +244,7 @@
 
 def filter_kernel(count, first, slot, spread, *refs):
     banks = refs[:count]
-    packet_ref, basis_ref, _, *outs, token_ref, bank, column, coh, spec, xs, norms, out_ref, bank_sems, out_sem = refs[count:]
+    packet_ref, basis_ref, *outs, token_ref, bank, column, coh, spec, xs, norms, out_ref, bank_sems, out_sem = refs[count:]
     half = PEERS * CAP
     loads = [pltpu.make_async_copy(banks[i], bank.at[i], bank_sems.at[i]) for i in range(count)]
     for load in loads:
@@ -325,11 +325,14 @@
         return 0
 
     lax.fori_loop(0, count, block, 0)
+    outs = outs[len(outs) - (PEERS if spread else 1) :]
     if spread:
         x, c = lax.axis_index("seg") // (NZ * NC), lax.axis_index("seg") % NC
         puts = [
             pltpu.make_async_copy(
-                out_ref.at[((x + dx) % NX) * NC + (c + dc) % NC], outs[dx * NC + dc], out_sem.at[dx * NC + dc]
+                out_ref.at[((x + dx) % NX) * NC + (c + dc) % NC],
+                outs[dx * NC + dc].at[pl.ds(slot, count)],
+                out_sem.at[dx * NC + dc],
             )
             for dx in range(NX)
             for dc in range(NC)
@@ -352,12 +355,12 @@
         functools.partial(filter_kernel, count, first, slot, spread),
         out_shape=[
             jax.ShapeDtypeStruct(shape, jnp.bfloat16)
-            for shape in ([(count, CAP, STEP)] * PEERS if spread else [(PEERS, total, CAP, STEP)])
+            for shape in ([(total, CAP, STEP)] * PEERS if spread else [(PEERS, total, CAP, STEP)])
         ]
         + [jax.ShapeDtypeStruct((8, 128), jnp.float32)],
-        in_specs=[any_space] * count + [vmem, vmem, any_space],
+        in_specs=[any_space] * count + [vmem, vmem] + [any_space] * len(before),
         out_specs=[any_space] * (PEERS if spread else 1) + [vmem],
-        input_output_aliases={count + 2: 0} if slot else {},
+        input_output_aliases={count + 2 + k: k for k in range(len(before))} if slot else {},
         scratch_shapes=[
             pltpu.VMEM((count, SLOTS, WIDE), jnp.bfloat16),
             pltpu.VMEM((128, PEERS), jnp.float32),
@@ -374,7 +377,7 @@
             flops=0 if spread else count * (3 << 30), bytes_accessed=1 << 20, transcendentals=0
         ),
         name=f"filter{count}_{first}",
-    )(*banks, packet, basis, before)
+    )(*banks, packet, basis, *before)
 
 
 def order_kernel(near_ref, *refs):
@@ -463,10 +466,10 @@
     ring(2)
 
     near_part, far_part = PARTS
-    rows, slot, token = place, 0, place
+    rows, slot, token = [place], 0, place
     for step in CALLS[near_part]:
         with jax.named_scope("filter"):
-            rows, token = filter_banks(
+            *rows, token = filter_banks(
                 [held[d] for d in step], slot * CAP, packet, basis, slot, len(near_part), rows
             )
         slot += len(step)
@@ -475,7 +478,7 @@
         ring(k + 1)
     with jax.named_scope("back"):
         near = lax.all_to_all(
-            rows.reshape(PEERS, slot * CAP, STEP),
+            rows[0].reshape(PEERS, slot * CAP, STEP),
             "seg",
             split_axis=0,
             concat_axis=0,
@@ -485,10 +488,20 @@
     m = len(far_part)
     token, late_basis = lax.optimization_barrier((token, basis))
     late_basis = stage(late_basis)
-    with jax.named_scope("filter"):
-        *pieces, token = filter_banks(
-            [held[d] for d in far_part], slot * CAP, packet, late_basis, 0, m, token, spread=True
-        )
+    pieces, done = [token], 0
+    for step in CALLS[far_part]:
+        with jax.named_scope("filter"):
+            *pieces, token = filter_banks(
+                [held[d] for d in step],
+                (slot + done) * CAP,
+                packet,
+                late_basis,
+                done,
+                m,
+                pieces,
+                spread=True,
+            )
+        done += len(step)
     with jax.named_scope("back"):
         for k in range(1, PEERS):
             dx, dc = divmod(k, NC)

time: 103 us -> 101 us (0.981)
  waiting for transfers between devices: 11.8 us -> 5.86 us
  starting transfers between devices: 28.4 us -> 31.5 us
    ppermute x1, waiting for transfers between devices: 3.82 us -> 0.01 us  [ring(): lax.ppermute(held[3][half:], 'seg', down)]
    ppermute x3, starting transfers between devices: 8.43 us -> 11.6 us  [ring(): held[k] = lax.ppermute(held[k - 1], 'seg', down)]
    ppermute x3, starting transfers between devices: 2.47 us -> 0.01 us  [ring(): held[-k] = lax.ppermute(held[1 - k], 'seg', up)]
    ppermute x1, starting transfers between devices: 0.55 us -> 2.79 us  [ring(): lax.ppermute(held[3][half:], 'seg', down)]
    ppermute x7, starting transfers between devices: 9.55 us -> 11.3 us  [per_device(): pieces[k] = lax.ppermute(pieces[k], 'seg', to)]
    ppermute x1, waiting for transfers between devices: 1.18 us -> 0.01 us  [ring(): lax.ppermute(held[-3][:half], 'seg', up)]
    pallas_call x3 -> x4, Pallas kernels: 33.3 us -> 34.3 us  [filter_banks(): pl.pallas_call(functools.partial(filter_kernel, count, first, slot, sprea...]
  transfers between devices with their start and end apart: 16 -> 16, of which waited for: 6 -> 4; matrix products, arithmetic and copies ran while one was open for 0% -> 0% of each run, Pallas kernels for 33% -> 35%
where the time goes in v3:
time: 101 us
  Pallas kernels  42.1 us (42%)
  starting transfers between devices  31.5 us (31%)
  blocking collectives  19.2 us (19%)
  waiting for transfers between devices  5.86 us (6%)
  local copies, waits for them, and re-layouts  2.24 us (2%)
    pallas_call x4, Pallas kernels, filter_banks(): pl.pallas_call(functools.partial(filter_kernel, count, first, slot, sprea...  34.3 us
    all_to_all x1, blocking collectives, per_device(): lax.all_to_all(packet, ('seg', 'det'), split_axis=0, concat_axis=0, tiled...  19.2 us
    ppermute x3, starting transfers between devices, ring(): held[k] = lax.ppermute(held[k - 1], 'seg', down)  11.6 us
    ppermute x7, starting transfers between devices, per_device(): pieces[k] = lax.ppermute(pieces[k], 'seg', to)  11.3 us
    all_to_all x1, starting transfers between devices, per_device(): lax.all_to_all(rows[0].reshape(PEERS, slot * CAP, STEP), 'seg', split_axi...  5.57 us
    ppermute x7, waiting for transfers between devices, per_device(): pieces[k] = lax.ppermute(pieces[k], 'seg', to)  5.24 us
    pallas_call x1, Pallas kernels, head(): pl.pallas_call(head_kernel, out_shape=[jax.ShapeDtypeStruct((SLOTS, WIDE)...  3.75 us
    pallas_call x1, Pallas kernels, order_rows(): pl.pallas_call(order_kernel, out_shape=jax.ShapeDtypeStruct((n, STEP), jn...  3.17 us
  transfers between devices with their start and end apart: 16, of which 4 were waited for; matrix products, arithmetic and copies ran while one was open for 0% of the time, Pallas kernels for 35%

profile of v3, /device:TPU:1, one launch (start us, length us, event | category | flops | bytes accessed | tf_op | source)
XLA Modules:
  0.0 101.1 jit_solution(1580914854001730850)
XLA Ops:
  0.0 3.8 %head.1 = (bf16[64,4096]{1,0:T(8,128)(2,1)}, f32[32,1,4224]{2,1,0:T(1,128)}, f32[8,512]{1,0:T(8,128)}) custom-call(s32[1,64]{1,0:T(1,128)} %dur_ref.1, s32[4]{0:T(128)} %delays_ref.1, bf16[64,4096]{1,0:T(8,128)(2,1)} %bitcast.23, f32[32,128]{1,0:T(8,128)} %bitcast.24, s32[1,512]{1,0:T(1,128)} %bitcast.25, s32[1,512]{1,0:T(1,128)} %slot_ref.1), custom_call_target="tpu_custom_call" | custom-call | flops 8589934592 | bytes 2097152 | tf_op jit(solution)/shard_map/head/head/pallas_call | solution.py:143
  3.8 6.4 %collective-permute-start = (bf16[64,4096]{1,0:T(8,128)(2,1)}, bf16[64,4096]{1,0:T(8,128)(2,1)S(1)}, u32[]{:S(2)}, u32[]{:S(2)}) collective-permute-start(bf16[64,4096]{1,0:T(8,128)(2,1)} %get-tuple-element.38.refs_0_), channel_id=1, source_target_pairs={{0,56},{4,60},{8,0},{12,4},{16,8},{20,12},{24,16},{28,20},{32,24},... | collective-permute-start | bytes 1572872 | tf_op jit(solution)/shard_map/ring/ppermute | solution.py:453
  10.2 0.0 collective-permute-start.1
  10.2 19.2 %all_to_all.10.packet_ref = f32[32,1,4224]{2,1,0:T(1,128)S(1)} all-to-all(f32[32,1,4224]{2,1,0:T(1,128)} %get-tuple-element.37), channel_id=1, replica_groups={{0,1,2,3,4,5,6,7,64,65,66,67,68,69,70,71,128,129,130,131,132,133,134,13..., dimensions={0} | all-to-all | bytes 1081344 | tf_op jit(solution)/shard_map/exchange/all_to_all | solution.py:461
  29.4 3.0 %collective-permute-start.2 = (bf16[64,4096]{1,0:T(8,128)(2,1)S(1)}, bf16[64,4096]{1,0:T(8,128)(2,1)S(1)}, u32[]{:S(2)}, u32[]{:S(2)}) collective-permute-start(bf16[64,4096]{1,0:T(8,128)(2,1)S(1)} %collective-permute-done.refs_2_), channel_id=1, source_target_pairs={{0,56},{4,60},{8,0},{12,4},{16,8},{20,12},{24,16},{28,20},{32,24},... | collective-permute-start | bytes 1572872 | tf_op jit(solution)/shard_map/ring/ppermute | solution.py:453
  32.4 0.0 collective-permute-start.3
  32.4 0.6 combine.1.refs_3_.refs_2_.refs_1_
  33.1 12.2 %filter3_0.1 = (bf16[8,5,16,1024]{3,2,1,0:T(8,128)(2,1)}, f32[8,128]{1,0:T(8,128)}) custom-call(bf16[64,4096]{1,0:T(8,128)(2,1)S(1)} %copy-done.3, bf16[64,4096]{1,0:T(8,128)(2,1)S(1)} %collective-permute-done.1.refs_1_, bf16[64,4096]{1,0:T(8,128)(2,1)S(1)} %collective-permute-done.refs_2_, f32[8,1,8320]{2,1,0:T(1,128)S(1)} %combine.1.refs_3_.refs_2_.refs_1_, ...), custom_call_target="tpu_custom_call" | custom-call | flops 9663676416 | bytes 1048576 | tf_op jit(solution)/shard_map/filter/filter3_0/pallas_call | solution.py:354
  45.2 0.0 collective-permute-done.2.refs_1_
  45.3 0.6 collective-permute-done.3.refs_0_
  45.9 2.1 %collective-permute-start.4 = (bf16[64,4096]{1,0:T(8,128)(2,1)S(1)}, bf16[64,4096]{1,0:T(8,128)(2,1)S(1)}, u32[]{:S(2)}, u32[]{:S(2)}) collective-permute-start(bf16[64,4096]{1,0:T(8,128)(2,1)S(1)} %collective-permute-done.2.refs_1_), channel_id=1, source_target_pairs={{0,56},{4,60},{8,0},{12,4},{16,8},{20,12},{24,16},{28,20},{32,24},... | collective-permute-start | bytes 1572872 | tf_op jit(solution)/shard_map/ring/ppermute | solution.py:453
  48.0 8.8 %filter2_48.1 = (bf16[8,5,16,1024]{3,2,1,0:T(8,128)(2,1)}, f32[8,128]{1,0:T(8,128)S(1)}) custom-call(bf16[64,4096]{1,0:T(8,128)(2,1)} %collective-permute-done.3.refs_0_, bf16[64,4096]{1,0:T(8,128)(2,1)S(1)} %collective-permute-done.2.refs_1_, f32[8,1,8320]{2,1,0:T(1,128)S(1)} %combine.1.refs_3_.refs_2_.refs_1_, ...), custom_call_target="tpu_custom_call", output_to_operand_aliasing={{0}: (4, {})} | custom-call | flops 6442450944 | bytes 1048576 | tf_op jit(solution)/shard_map/filter/filter2_48/pallas_call | solution.py:354
  56.9 5.6 %all-to-all-start.1 = ((bf16[8,80,1024]{2,1,0:T(8,128)(2,1)}), bf16[8,80,1024]{2,1,0:T(8,128)(2,1)S(1)}, u32[]{:S(2)}, u32[]{:S(2)}) async-start(bf16[8,80,1024]{2,1,0:T(8,128)(2,1)} %bitcast.3), calls=%async_computation.1 | async-start | bytes 2621440 | tf_op jit(solution)/shard_map/back/all_to_all | solution.py:480
  62.4 0.0 collective-permute-done.4.refs_1_
  62.4 0.0 collective-permute-done.5.refs_0_
  62.5 0.3 collective-permute-start.6
  62.8 2.8 %collective-permute-start.7 = (bf16[32,4096]{1,0:T(8,128)(2,1)S(1)}, bf16[32,4096]{1,0:T(8,128)(2,1)S(1)}, u32[]{:S(2)}, u32[]{:S(2)}) collective-permute-start(bf16[32,4096]{1,0:T(8,128)(2,1)S(1)} %slice.7), channel_id=1, source_target_pairs={{0,56},{4,60},{8,0},{12,4},{16,8},{20,12},{24,16},{28,20},{32,24},... | collective-permute-start | bytes 786440 | tf_op jit(solution)/shard_map/ring/ppermute | solution.py:456
  65.6 2.2 %copy-done.1 = bf16[16,256,512]{2,1,0:T(8,128)(2,1)S(1)} copy-done((bf16[16,256,512]{2,1,0:T(8,128)(2,1)S(1)}, bf16[16,256,512]{2,1,0:T(8,128)(2,1)}, u32[]{:S(2)}) %copy-start.1) | copy-done | bytes 4194328
  67.8 0.3 stage_basis.1.refs_3_.refs_2_
  68.0 8.6 %filter2_80.1 = (bf16[3,16,1024]{2,1,0:T(8,128)(2,1)S(1)}, bf16[3,16,1024]{2,1,0:T(8,128)(2,1)S(1)}, bf16[3,16,1024]{2,1,0:T(8,128)(2,1)S(1)}, bf16[3,16,1024]{2...) custom-call(bf16[64,4096]{1,0:T(8,128)(2,1)S(1)} %collective-permute, ...), custom_call_target="tpu_custom_call" | custom-call | bytes 1048576 | tf_op jit(solution)/shard_map/filter/filter2_80/pallas_call | solution.py:354
  76.7 0.0 collective-permute-done.7
  76.7 4.7 %filter1_112.1 = (bf16[3,16,1024]{2,1,0:T(8,128)(2,1)S(1)}, bf16[3,16,1024]{2,1,0:T(8,128)(2,1)S(1)}, bf16[3,16,1024]{2,1,0:T(8,128)(2,1)S(1)}, bf16[3,16,1024]{...) custom-call(bf16[64,4096]{1,0:T(8,128)(2,1)S(1)} %pad_maximum_fusion, ...), custom_call_target="tpu_custom_call", output_to_operand_aliasing={{0}: (3, {}), {1}: (4, {}), {2}: (5, {}), {3}: (6, {}), {4}... | custom-call | bytes 1048576 | tf_op jit(solution)/shard_map/filter/filter1_112/pallas_call | solution.py:354
  81.4 3.7 %collective-permute-start.12 = (bf16[3,16,1024]{2,1,0:T(8,128)(2,1)S(1)}, bf16[3,16,1024]{2,1,0:T(8,128)(2,1)S(1)}, u32[]{:S(2)}, u32[]{:S(2)}) collective-permute-start(bf16[3,16,1024]{2,1,0:T(8,128)(2,1)S(1)} %get-tuple-element.66), channel_id=1, source_target_pairs={{0,132},{4,128},{8,140},{12,136},{16,148},{20,144},{24,156},{28,15... | collective-permute-start | bytes 294920 | tf_op jit(solution)/shard_map/back/ppermute | solution.py:509
  85.2 1.2 %collective-permute-start.13 = (bf16[3,16,1024]{2,1,0:T(8,128)(2,1)S(1)}, bf16[3,16,1024]{2,1,0:T(8,128)(2,1)S(1)}, u32[]{:S(2)}, u32[]{:S(2)}) collective-permute-start(bf16[3,16,1024]{2,1,0:T(8,128)(2,1)S(1)} %get-tuple-element.67), channel_id=1, source_target_pairs={{0,192},{4,196},{8,200},{12,204},{16,208},{20,212},{24,216},{28,22... | collective-permute-start | bytes 294920 | tf_op jit(solution)/shard_map/back/ppermute | solution.py:509
  86.3 0.5 collective-permute-start.8
  86.9 1.3 %collective-permute-start.9 = (bf16[3,16,1024]{2,1,0:T(8,128)(2,1)S(1)}, bf16[3,16,1024]{2,1,0:T(8,128)(2,1)S(1)}, u32[]{:S(2)}, u32[]{:S(2)}) collective-permute-start(bf16[3,16,1024]{2,1,0:T(8,128)(2,1)S(1)} %get-tuple-element.63), channel_id=1, source_target_pairs={{0,64},{4,68},{8,72},{12,76},{16,80},{20,84},{24,88},{28,92},{32,9... | collective-permute-start | bytes 294920 | tf_op jit(solution)/shard_map/back/ppermute | solution.py:509
  88.2 2.3 %collective-permute-start.10 = (bf16[3,16,1024]{2,1,0:T(8,128)(2,1)S(1)}, bf16[3,16,1024]{2,1,0:T(8,128)(2,1)S(1)}, u32[]{:S(2)}, u32[]{:S(2)}) collective-permute-start(bf16[3,16,1024]{2,1,0:T(8,128)(2,1)S(1)} %get-tuple-element.64), channel_id=1, source_target_pairs={{0,68},{4,64},{8,76},{12,72},{16,84},{20,80},{24,92},{28,88},{32,1... | collective-permute-start | bytes 294920 | tf_op jit(solution)/shard_map/back/ppermute | solution.py:509
  90.5 0.2 collective-permute-done.13
  90.6 2.2 %collective-permute-start.11 = (bf16[3,16,1024]{2,1,0:T(8,128)(2,1)S(1)}, bf16[3,16,1024]{2,1,0:T(8,128)(2,1)S(1)}, u32[]{:S(2)}, u32[]{:S(2)}) collective-permute-start(bf16[3,16,1024]{2,1,0:T(8,128)(2,1)S(1)} %get-tuple-element.65), channel_id=1, source_target_pairs={{0,128},{4,132},{8,136},{12,140},{16,144},{20,148},{24,152},{28,15... | collective-permute-start | bytes 294920 | tf_op jit(solution)/shard_map/back/ppermute | solution.py:509
  92.9 2.2 %collective-permute-done.10 = bf16[3,16,1024]{2,1,0:T(8,128)(2,1)S(1)} collective-permute-done((bf16[3,16,1024]{2,1,0:T(8,128)(2,1)S(1)}, bf16[3,16,1024]{2,1,0:T(8,128)(2,1)S(1)}, u32[]{:S(2)}, u32[]{:S(2)}) %collective-permute-start.10) | collective-permute-done | bytes 98336 | tf_op jit(solution)/shard_map/back/ppermute | solution.py:509
  95.1 2.9 %collective-permute-done.11 = bf16[3,16,1024]{2,1,0:T(8,128)(2,1)S(1)} collective-permute-done((bf16[3,16,1024]{2,1,0:T(8,128)(2,1)S(1)}, bf16[3,16,1024]{2,1,0:T(8,128)(2,1)S(1)}, u32[]{:S(2)}, u32[]{:S(2)}) %collective-permute-start.11) | collective-permute-done | bytes 98336 | tf_op jit(solution)/shard_map/back/ppermute | solution.py:509
  97.9 3.2 %order_rows.1 = f32[512,1024]{1,0:T(8,128)} custom-call(bf16[640,1024]{1,0:T(8,128)(2,1)S(1)} %bitcast.14, bf16[48,1024]{1,0:T(8,128)(2,1)S(1)} %bitcast.15, bf16[48,1024]{1,0:T(8,128)(2,1)S(1)} %bitcast.19, bf16[48,1024]{1,0:T(8,128)(2,1)S(1)} %bitcast.20, bf16[48,1024]{1,0:T(8,128)(2,1)S(1)} %bitcast.21, bf16[48,1024]{1,0:T(8,128)(2,1)S(1)} %bitcast.22, ...), custom_call_target="tpu_custom_call" | custom-call | flops 1073741824 | bytes 4194304 | tf_op jit(solution)/shard_map/order/order_rows/pallas_call | solution.py:412
  (22 shorter events, 0.1 us)
Async XLA Ops:
  0.0 32.4 %copy-start.4 = (f32[2,4]{1,0:T(2,128)S(1)}, f32[2,4]{1,0:T(2,128)}, u32[]{:S(2)}) copy-start(f32[2,4]{1,0:T(2,128)} %antenna_ref.1) | copy-start | bytes 100
  3.8 25.6 %collective-permute-start = (bf16[64,4096]{1,0:T(8,128)(2,1)}, bf16[64,4096]{1,0:T(8,128)(2,1)S(1)}, u32[]{:S(2)}, u32[]{:S(2)}) collective-permute-start(bf16[64,4096]{1,0:T(8,128)(2,1)} %get-tuple-element.38.refs_0_), channel_id=1, source_target_pairs={{0,56},{4,60},{8,0},{12,4},{16,8},{20,12},{24,16},{28,20},{32,24},... | collective-permute-start | bytes 1572872 | tf_op jit(solution)/shard_map/ring/ppermute | solution.py:453
  10.2 19.2 %collective-permute-start.1 = (bf16[64,4096]{1,0:T(8,128)(2,1)}, bf16[64,4096]{1,0:T(8,128)(2,1)S(1)}, u32[]{:S(2)}, u32[]{:S(2)}) collective-permute-start(bf16[64,4096]{1,0:T(8,128)(2,1)} %get-tuple-element.38.refs_0_), channel_id=1, source_target_pairs={{0,8},{4,12},{8,16},{12,20},{16,24},{20,28},{24,32},{28,36},{32,40... | collective-permute-start | bytes 1572872 | tf_op jit(solution)/shard_map/ring/ppermute | solution.py:452
  29.4 3.7 %copy-start = (bf16[16,256,512]{2,1,0:T(8,128)(2,1)S(1)}, bf16[16,256,512]{2,1,0:T(8,128)(2,1)}, u32[]{:S(2)}) copy-start(bf16[16,256,512]{2,1,0:T(8,128)(2,1)} %constant.2.clone.refs_4_.refs_3_.source) | copy-start | bytes 12582916
  29.4 3.7 %copy-start.2 = (f32[8,512]{1,0:T(8,128)S(1)}, f32[8,512]{1,0:T(8,128)}, u32[]{:S(2)}) copy-start(f32[8,512]{1,0:T(8,128)} %get-tuple-element.44.refs_5_.refs_8_) | copy-start | bytes 49156
  29.4 3.7 %copy-start.3 = (bf16[64,4096]{1,0:T(8,128)(2,1)S(1)}, bf16[64,4096]{1,0:T(8,128)(2,1)}, u32[]{:S(2)}) copy-start(bf16[64,4096]{1,0:T(8,128)(2,1)} %get-tuple-element.38.refs_0_) | copy-start | bytes 1572868
  29.4 15.9 %collective-permute-start.2 = (bf16[64,4096]{1,0:T(8,128)(2,1)S(1)}, bf16[64,4096]{1,0:T(8,128)(2,1)S(1)}, u32[]{:S(2)}, u32[]{:S(2)}) collective-permute-start(bf16[64,4096]{1,0:T(8,128)(2,1)S(1)} %collective-permute-done.refs_2_), channel_id=1, source_target_pairs={{0,56},{4,60},{8,0},{12,4},{16,8},{20,12},{24,16},{28,20},{32,24},... | collective-permute-start | bytes 1572872 | tf_op jit(solution)/shard_map/ring/ppermute | solution.py:453
  32.4 13.4 %collective-permute-start.3 = (bf16[64,4096]{1,0:T(8,128)(2,1)S(1)}, bf16[64,4096]{1,0:T(8,128)(2,1)}, u32[]{:S(2)}, u32[]{:S(2)}) collective-permute-start(bf16[64,4096]{1,0:T(8,128)(2,1)S(1)} %collective-permute-done.1.refs_1_), channel_id=1, source_target_pairs={{0,8},{4,12},{8,16},{12,20},{16,24},{20,28},{24,32},{28,36},{32,40... | collective-permute-start | bytes 1572872 | tf_op jit(solution)/shard_map/ring/ppermute | solution.py:452
  45.9 16.6 %collective-permute-start.4 = (bf16[64,4096]{1,0:T(8,128)(2,1)S(1)}, bf16[64,4096]{1,0:T(8,128)(2,1)S(1)}, u32[]{:S(2)}, u32[]{:S(2)}) collective-permute-start(bf16[64,4096]{1,0:T(8,128)(2,1)S(1)} %collective-permute-done.2.refs_1_), channel_id=1, source_target_pairs={{0,56},{4,60},{8,0},{12,4},{16,8},{20,12},{24,16},{28,20},{32,24},... | collective-permute-start | bytes 1572872 | tf_op jit(solution)/shard_map/ring/ppermute | solution.py:453
  48.0 14.4 %collective-permute-start.5 = (bf16[64,4096]{1,0:T(8,128)(2,1)}, bf16[64,4096]{1,0:T(8,128)(2,1)S(1)}, u32[]{:S(2)}, u32[]{:S(2)}) collective-permute-start(bf16[64,4096]{1,0:T(8,128)(2,1)} %collective-permute-done.3.refs_0_), channel_id=1, source_target_pairs={{0,8},{4,12},{8,16},{12,20},{16,24},{20,28},{24,32},{28,36},{32,40... | collective-permute-start | bytes 1572872 | tf_op jit(solution)/shard_map/ring/ppermute | solution.py:452
  56.9 41.1 %all-to-all-start.1 = ((bf16[8,80,1024]{2,1,0:T(8,128)(2,1)}), bf16[8,80,1024]{2,1,0:T(8,128)(2,1)S(1)}, u32[]{:S(2)}, u32[]{:S(2)}) async-start(bf16[8,80,1024]{2,1,0:T(8,128)(2,1)} %bitcast.3), calls=%async_computation.1 | async-start | bytes 2621440 | tf_op jit(solution)/shard_map/back/all_to_all | solution.py:480
  62.5 14.2 %collective-permute-start.6 = (bf16[32,4096]{1,0:T(8,128)(2,1)S(1)}, bf16[32,4096]{1,0:T(8,128)(2,1)S(1)}, u32[]{:S(2)}, u32[]{:S(2)}) collective-permute-start(bf16[32,4096]{1,0:T(8,128)(2,1)S(1)} %slice.6), channel_id=1, source_target_pairs={{0,8},{4,12},{8,16},{12,20},{16,24},{20,28},{24,32},{28,36},{32,40... | collective-permute-start | bytes 786440 | tf_op jit(solution)/shard_map/ring/ppermute | solution.py:456
  62.8 13.9 %collective-permute-start.7 = (bf16[32,4096]{1,0:T(8,128)(2,1)S(1)}, bf16[32,4096]{1,0:T(8,128)(2,1)S(1)}, u32[]{:S(2)}, u32[]{:S(2)}) collective-permute-start(bf16[32,4096]{1,0:T(8,128)(2,1)S(1)} %slice.7), channel_id=1, source_target_pairs={{0,56},{4,60},{8,0},{12,4},{16,8},{20,12},{24,16},{28,20},{32,24},... | collective-permute-start | bytes 786440 | tf_op jit(solution)/shard_map/ring/ppermute | solution.py:456
  65.6 2.2 %copy-start.1 = (bf16[16,256,512]{2,1,0:T(8,128)(2,1)S(1)}, bf16[16,256,512]{2,1,0:T(8,128)(2,1)}, u32[]{:S(2)}) copy-start(bf16[16,256,512]{2,1,0:T(8,128)(2,1)} %constant.2.clone.refs_4_.refs_3_.source) | copy-start | bytes 12582916
  81.4 6.8 %collective-permute-start.12 = (bf16[3,16,1024]{2,1,0:T(8,128)(2,1)S(1)}, bf16[3,16,1024]{2,1,0:T(8,128)(2,1)S(1)}, u32[]{:S(2)}, u32[]{:S(2)}) collective-permute-start(bf16[3,16,1024]{2,1,0:T(8,128)(2,1)S(1)} %get-tuple-element.66), channel_id=1, source_target_pairs={{0,132},{4,128},{8,140},{12,136},{16,148},{20,144},{24,156},{28,15... | collective-permute-start | bytes 294920 | tf_op jit(solution)/shard_map/back/ppermute | solution.py:509
  85.2 5.5 %collective-permute-start.13 = (bf16[3,16,1024]{2,1,0:T(8,128)(2,1)S(1)}, bf16[3,16,1024]{2,1,0:T(8,128)(2,1)S(1)}, u32[]{:S(2)}, u32[]{:S(2)}) collective-permute-start(bf16[3,16,1024]{2,1,0:T(8,128)(2,1)S(1)} %get-tuple-element.67), channel_id=1, source_target_pairs={{0,192},{4,196},{8,200},{12,204},{16,208},{20,212},{24,216},{28,22... | collective-permute-start | bytes 294920 | tf_op jit(solution)/shard_map/back/ppermute | solution.py:509
  86.3 6.6 %collective-permute-start.14 = (bf16[3,16,1024]{2,1,0:T(8,128)(2,1)S(1)}, bf16[3,16,1024]{2,1,0:T(8,128)(2,1)S(1)}, u32[]{:S(2)}, u32[]{:S(2)}) collective-permute-start(bf16[3,16,1024]{2,1,0:T(8,128)(2,1)S(1)} %get-tuple-element.68), channel_id=1, source_target_pairs={{0,196},{4,192},{8,204},{12,200},{16,212},{20,208},{24,220},{28,21... | collective-permute-start | bytes 294920 | tf_op jit(solution)/shard_map/back/ppermute | solution.py:509
  86.3 6.6 %collective-permute-start.8 = (bf16[3,16,1024]{2,1,0:T(8,128)(2,1)S(1)}, bf16[3,16,1024]{2,1,0:T(8,128)(2,1)S(1)}, u32[]{:S(2)}, u32[]{:S(2)}) collective-permute-start(bf16[3,16,1024]{2,1,0:T(8,128)(2,1)S(1)} %get-tuple-element.62), channel_id=1, source_target_pairs={{0,4},{4,0},{8,12},{12,8},{16,20},{20,16},{24,28},{28,24},{32,36},... | collective-permute-start | bytes 294920 | tf_op jit(solution)/shard_map/back/ppermute | solution.py:509
  86.9 6.0 %collective-permute-start.9 = (bf16[3,16,1024]{2,1,0:T(8,128)(2,1)S(1)}, bf16[3,16,1024]{2,1,0:T(8,128)(2,1)S(1)}, u32[]{:S(2)}, u32[]{:S(2)}) collective-permute-start(bf16[3,16,1024]{2,1,0:T(8,128)(2,1)S(1)} %get-tuple-element.63), channel_id=1, source_target_pairs={{0,64},{4,68},{8,72},{12,76},{16,80},{20,84},{24,88},{28,92},{32,9... | collective-permute-start | bytes 294920 | tf_op jit(solution)/shard_map/back/ppermute | solution.py:509
  88.2 6.9 %collective-permute-start.10 = (bf16[3,16,1024]{2,1,0:T(8,128)(2,1)S(1)}, bf16[3,16,1024]{2,1,0:T(8,128)(2,1)S(1)}, u32[]{:S(2)}, u32[]{:S(2)}) collective-permute-start(bf16[3,16,1024]{2,1,0:T(8,128)(2,1)S(1)} %get-tuple-element.64), channel_id=1, source_target_pairs={{0,68},{4,64},{8,76},{12,72},{16,84},{20,80},{24,92},{28,88},{32,1... | collective-permute-start | bytes 294920 | tf_op jit(solution)/shard_map/back/ppermute | solution.py:509
  90.6 7.3 %collective-permute-start.11 = (bf16[3,16,1024]{2,1,0:T(8,128)(2,1)S(1)}, bf16[3,16,1024]{2,1,0:T(8,128)(2,1)S(1)}, u32[]{:S(2)}, u32[]{:S(2)}) collective-permute-start(bf16[3,16,1024]{2,1,0:T(8,128)(2,1)S(1)} %get-tuple-element.65), channel_id=1, source_target_pairs={{0,128},{4,132},{8,136},{12,140},{16,144},{20,148},{24,152},{28,15... | collective-permute-start | bytes 294920 | tf_op jit(solution)/shard_map/back/ppermute | solution.py:509
